TPU v7x, 128 devices: a whole 4x4x4 slice. The times are simulated.
128 devices in a mesh: col: 8 (over z, core), row: 16 (over x, y).
Axes of the slice: x: 4, y: 4, z: 4, core: 2. Of those that a mesh axis runs over, the one named last changes fastest.
Arguments:
- block_pixels: float32 [16384, 8, 256], P(('col', 'row')), may hold values from -6 to 6
- block_ivar: bfloat16 [16384, 8, 256], P(('col', 'row')), may hold values from 0.29882812 to 3
- block_mask: int32 [16384, 8, 256], P(('col', 'row')), may hold values 0 or 1
- block_patch: int32 [16384, 1], P(('col', 'row')), may hold values from 0 to 127; in each aligned block of 128 rows (0 to 127, 128 to 255, ...) at most 2 rows name the same one
- block_offset: int32 [16384], P(('col', 'row')), may hold values from 0 to 120
- block_exposure: int32 [16384], P(('col', 'row')), may hold values from 0 to 95
- exposure_band: int32 [96], replicated, may hold values from 0 to 5
- basis: float32 [5, 41, 41], replicated, may hold values from -0.15625 to 0.15625
- coefficients: float32 [16, 8, 6, 5], P('row', 'col'), may hold values from -3 to 3
Outputs:
- coadd: float32 [6, 2048, 2048], P(None, 'row', 'col')
Inputs may be any that keep to these rules, and one draw needn't show every extreme that they name: `block_patch`: among the blocks of one device at most 2 name the same patch, a bound that some block reaches.
All inputs are finite; a program needn't handle non-finite values. No bound on the sum of `block_mask` on one device may be relied on, other than what follows from the above.
Results may differ from a plain program's by a relative error of at most 0.0049.
Values may be sent and summed in bfloat16 or wider, within the bound.
A program may use at most 64 MiB of HBM per device.

v0:
```python
import jax
import jax.numpy as jnp
from jax import lax
from jax.sharding import PartitionSpec as P

BANDS = 6
KS = 41
HALF = 20
PH = 128


def extended(block, sides, width):
    for axis, dim in sides:
        count = lax.axis_size(axis)
        forward = [(i, i + 1) for i in range(count - 1)]
        backward = [(target, source) for source, target in forward]
        low = lax.ppermute(
            lax.slice_in_dim(block, block.shape[dim] - width, None, axis=dim), axis, forward
        )
        high = lax.ppermute(lax.slice_in_dim(block, 0, width, axis=dim), axis, backward)
        block = jnp.concatenate([low, block, high], axis=dim)
    return block


def on_device(
    block_pixels,
    block_ivar,
    block_mask,
    block_patch,
    block_offset,
    block_exposure,
    exposure_band,
    basis,
    coefficients,
):
    nblocks, block_rows, patch_cols = block_pixels.shape
    col_count = lax.axis_size("col")
    row_count = lax.axis_size("row")
    device_count = col_count * row_count
    capacity = 2 * nblocks // device_count
    weight = block_mask.astype(jnp.float32) * block_ivar.astype(jnp.float32)
    payload = jnp.stack(
        [(weight * block_pixels).astype(jnp.bfloat16), weight.astype(jnp.bfloat16)], axis=2
    )
    target = block_patch[:, 0]
    positions = jnp.arange(nblocks, dtype=jnp.int32)
    earlier = (target[:, None] == target[None, :]) & (positions[None, :] < positions[:, None])
    rank_ids = jnp.sum(earlier.astype(jnp.int32), axis=1)
    slot_ids = target * capacity + rank_ids
    exposure_ids = jnp.arange(exposure_band.shape[0], dtype=jnp.int32)
    band_ids = jnp.sum(
        jnp.where(block_exposure[:, None] == exposure_ids[None, :], exposure_band[None, :], 0),
        axis=1,
    )
    labels = jnp.stack([block_offset, band_ids], axis=1)
    slots = device_count * capacity
    slot_match = jnp.arange(slots, dtype=jnp.int32)[:, None] == slot_ids[None, :]
    onehot = slot_match.astype(jnp.bfloat16)
    send_flat = jnp.dot(
        onehot,
        payload.reshape(nblocks, block_rows * 2 * patch_cols),
        preferred_element_type=jnp.float32,
    )
    send_data = send_flat.astype(jnp.bfloat16).reshape((slots, block_rows, 2, patch_cols))
    filled = jnp.any(slot_match, axis=1)
    picked = jnp.sum(jnp.where(slot_match[:, :, None], labels[None, :, :], 0), axis=1)
    send_labels = jnp.where(filled[:, None], picked, -1)
    got_data, got_labels = (
        lax.all_to_all(send_data, ("col", "row"), split_axis=0, concat_axis=0, tiled=True),
        lax.all_to_all(send_labels, ("col", "row"), split_axis=0, concat_axis=0, tiled=True),
    )
    flat_data = got_data.reshape(slots * block_rows, 2 * patch_cols)
    got_offsets = got_labels[:, 0]
    got_bands = got_labels[:, 1]
    band_match = (
        got_bands[None, None, :, None] == jnp.arange(BANDS, dtype=jnp.int32)[:, None, None, None]
    )
    row_match = (
        got_offsets[None, None, :, None]
        + jnp.arange(block_rows, dtype=jnp.int32)[None, None, None, :]
        == jnp.arange(PH, dtype=jnp.int32)[None, :, None, None]
    )
    placement = (
        (band_match & row_match).astype(jnp.bfloat16).reshape(BANDS * PH, slots * block_rows)
    )
    sums = jnp.dot(placement, flat_data, preferred_element_type=jnp.float32).reshape(
        BANDS, PH, 2, patch_cols
    )
    mean_image = (sums[:, :, 0, :] / jnp.maximum(sums[:, :, 1, :], 1.0)).astype(jnp.bfloat16)
    padded = extended(mean_image, (("col", 2), ("row", 1)), HALF)
    kernel = jnp.einsum(
        "bk,kij->bij", coefficients[0, 0], basis, precision=lax.Precision.HIGHEST
    ).astype(jnp.bfloat16)
    wide_cols = patch_cols + 2 * HALF
    wide_rows = PH + 2 * HALF
    table = (
        jnp.arange(wide_cols, dtype=jnp.int32)[None, :, None]
        - jnp.arange(patch_cols, dtype=jnp.int32)[None, None, :]
        == jnp.arange(KS, dtype=jnp.int32)[:, None, None]
    ).astype(jnp.bfloat16)

    def convolve(pair):
        image, taps = pair
        toeplitz = jnp.einsum(
            "dk,kpx->pdx", taps, table, preferred_element_type=jnp.float32
        ).astype(jnp.bfloat16)
        spread = jnp.dot(
            image, toeplitz.reshape(wide_cols, KS * patch_cols), preferred_element_type=jnp.float32
        )
        spread = spread.reshape(wide_rows, KS, patch_cols)
        total = spread[0:PH, 0, :]
        for offset_y in range(1, KS):
            total = total + spread[offset_y : offset_y + PH, offset_y, :]
        return total

    return lax.map(convolve, (padded, kernel))


def solution(mesh):
    placed = (
        P(("col", "row"), None, None),
        P(("col", "row"), None, None),
        P(("col", "row"), None, None),
        P(("col", "row"), None),
        P(("col", "row")),
        P(("col", "row")),
        P(),
        P(),
        P("row", "col", None, None),
    )
    return jax.shard_map(
        on_device, mesh=mesh, in_specs=placed, out_specs=P(None, "row", "col"), check_vma=False
    )
```

profile of v0, /device:TPU:1, one launch (start us, length us, event | category | flops | bytes accessed | tf_op | source)
XLA Modules:
  0.0 132.9 jit_solution(12044168816160134304)
XLA Ops:
  0.0 0.0 copy-start
  0.0 0.9 convert_reduce_fusion
  0.9 0.7 multiply_add_fusion
  1.6 0.1 fusion.56
  1.7 0.8 select_reduce_fusion.1
  2.5 0.7 pad_add_fusion
  3.2 0.1 select_reduce_fusion
  3.3 0.1 reduce_sum.32
  3.5 0.2 broadcast_in_dim.68
  3.6 0.8 copy.48
  4.4 11.5 %all-to-all-start = ((s32[128,2,2]{1,2,0:T(2,128)}), s32[128,2,2]{1,2,0:T(2,128)S(1)}, u32[]{:S(2)}, u32[]{:S(2)}) async-start(s32[128,2,2]{1,2,0:T(2,128)} %copy.48), calls=%async_computation | async-start | bytes 262144 | tf_op jit(solution)/shard_map/all_to_all | solution.py:70
  15.9 1.6 %copy.50 = s32[128,8,256]{0,2,1:T(8,128)S(1)} copy(s32[128,8,256]{2,1,0:T(8,128)} %param.13) | data formatting | bytes 2097152 | tf_op args[2]
  17.5 0.0 copy-done.1
  17.5 0.4 copy.52
  17.9 1.5 %copy.51 = bf16[128,8,256]{0,2,1:T(8,128)(2,1)S(1)} copy(bf16[128,8,256]{2,1,0:T(8,128)(2,1)} %param.12) | data formatting | bytes 1048576 | tf_op args[1]
  19.4 0.3 fusion.53
  19.7 0.1 pad_maximum_fusion
  19.8 0.7 convolution_convert_fusion
  20.5 2.8 %reshape.559 = bf16[256,8,2,256]{3,2,1,0:T(2,128)(2,1)} reshape(bf16[256,4096]{1,0:T(8,128)(2,1)S(1)} %convolution_convert_fusion) | data formatting | bytes 4194304 | tf_op jit(solution)/shard_map/reshape | solution.py:64
  23.3 2.7 %all-to-all-done = s32[128,2,2]{1,2,0:T(2,128)S(1)} async-done(((s32[128,2,2]{1,2,0:T(2,128)}), s32[128,2,2]{1,2,0:T(2,128)S(1)}, u32[]{:S(2)}, u32[]{:S(2)}) %all-to-all-start) | async-done | bytes 2080 | tf_op jit(solution)/shard_map/all_to_all | solution.py:70
  26.0 7.1 %all-to-all-start.1 = ((bf16[256,8,2,256]{3,2,1,0:T(2,128)(2,1)}), bf16[256,8,2,256]{3,2,1,0:T(2,128)(2,1)S(1)}, u32[]{:S(2)}, u32[]{:S(2)}) async-start(bf16[256,8,2,256]{3,2,1,0:T(2,128)(2,1)} %reshape.559), calls=%async_computation.1 | async-start | bytes 4194304 | tf_op jit(solution)/shard_map/all_to_all | solution.py:69
  33.0 0.1 copy.55
  33.1 0.1 all_to_all.10
  33.3 0.1 iota_add_fusion
  33.4 0.1 add.445
  33.5 0.3 and.25
  33.8 0.5 and.26
  34.3 0.1 iota_compare_fusion.1
  34.4 28.4 %all-to-all-done.1 = bf16[256,8,2,256]{3,2,1,0:T(2,128)(2,1)S(1)} async-done(((bf16[256,8,2,256]{3,2,1,0:T(2,128)(2,1)}), bf16[256,8,2,256]{3,2,1,0:T(2,128)(2,1)S(1)}, u32[]{:S(2)}, u32[]{:S(2)}) %all-to-all-start.1) | async-done | bytes 2097184 | tf_op jit(solution)/shard_map/all_to_all | solution.py:69
  62.8 1.9 %copy.61 = bf16[256,8,2,256]{3,1,2,0:T(8,128)(2,1)} copy(bf16[256,8,2,256]{3,2,1,0:T(2,128)(2,1)S(1)} %all-to-all-done.1) | data formatting | bytes 4194304
  64.7 2.9 %copy.54 = bf16[2048,512]{0,1:T(8,128)(2,1)S(1)} copy(bf16[2048,512]{1,0:T(8,128)(2,1)} %bitcast.268) | data formatting | bytes 4194304 | tf_op jit(solution)/shard_map/reshape | solution.py:72
  67.6 1.8 %fusion.44 = f32[6,128,2,256]{3,1,2,0:T(8,128)S(1)} fusion(bf16[2,256,2048,1]{2,1,0,3:T(8,128)(2,1)S(1)} %bitcast.270, pred[128,2048]{1,0:T(8,128)(4,1)S(1)} %iota_compare_fusion.1, pred[6,2048]{1,0:T(8,128)(4,1)S(1)} %and.26), kind=kOutput, calls=%fused_computation.81 | convolution fusion | flops 1612185600 | bytes 3944448 | tf_op jit(solution)/shard_map/dot_general | solution.py:86
  69.4 0.1 fusion.54
  69.6 0.1 fusion.60
  69.7 3.4 %collective-permute-start = (bf16[6,128,20]{2,1,0:T(8,128)(2,1)S(1)}, bf16[6,128,20]{2,1,0:T(8,128)(2,1)S(1)}, u32[]{:S(2)}, u32[]{:S(2)}) collective-permute-start(bf16[6,128,20]{2,1,0:T(8,128)(2,1)S(1)} %get-tuple-element.85), channel_id=1, source_target_pairs={{0,16},{16,32},{32,48},{48,64},{64,80},{80,96},{96,112},{1,17},{17... | collective-permute-start | bytes 92168 | tf_op jit(solution)/shard_map/ppermute | solution.py:17
  73.1 1.9 %collective-permute-start.1 = (bf16[6,128,20]{2,1,0:T(8,128)(2,1)S(1)}, bf16[6,128,20]{2,1,0:T(8,128)(2,1)S(1)}, u32[]{:S(2)}, u32[]{:S(2)}) collective-permute-start(bf16[6,128,20]{2,1,0:T(8,128)(2,1)S(1)} %get-tuple-element.86), channel_id=1, source_target_pairs={{16,0},{32,16},{48,32},{64,48},{80,64},{96,80},{112,96},{17,1},{33... | collective-permute-start | bytes 92168 | tf_op jit(solution)/shard_map/ppermute | solution.py:20
  75.0 0.3 convolution_convert_fusion.1
  75.3 0.3 collective-permute-done
  75.7 4.4 %collective-permute-done.1 = bf16[6,128,20]{2,1,0:T(8,128)(2,1)S(1)} collective-permute-done((bf16[6,128,20]{2,1,0:T(8,128)(2,1)S(1)}, bf16[6,128,20]{2,1,0:T(8,128)(2,1)S(1)}, u32[]{:S(2)}, u32[]{:S(2)}) %collective-permute-start.1) | collective-permute-done | bytes 30752 | tf_op jit(solution)/shard_map/ppermute | solution.py:20
  80.0 0.2 pad_maximum_fusion.4
  80.2 2.6 %collective-permute-start.2 = (bf16[6,20,296]{2,1,0:T(8,128)(2,1)S(1)}, bf16[6,20,296]{2,1,0:T(8,128)(2,1)S(1)}, u32[]{:S(2)}, u32[]{:S(2)}) collective-permute-start(bf16[6,20,296]{2,1,0:T(8,128)(2,1)S(1)} %get-tuple-element.83), channel_id=1, source_target_pairs={{0,1},{1,2},{2,3},{3,4},{4,5},{5,6},{6,7},{7,8},{8,9},{9,10},{10,1... | collective-permute-start | bytes 213128 | tf_op jit(solution)/shard_map/ppermute | solution.py:17
  82.8 1.5 %collective-permute-start.3 = (bf16[6,20,296]{2,1,0:T(8,128)(2,1)S(1)}, bf16[6,20,296]{2,1,0:T(8,128)(2,1)S(1)}, u32[]{:S(2)}, u32[]{:S(2)}) collective-permute-start(bf16[6,20,296]{2,1,0:T(8,128)(2,1)S(1)} %get-tuple-element.84), channel_id=1, source_target_pairs={{1,0},{2,1},{3,2},{4,3},{5,4},{6,5},{7,6},{8,7},{9,8},{10,9},{11,1... | collective-permute-start | bytes 213128 | tf_op jit(solution)/shard_map/ppermute | solution.py:20
  84.3 0.2 collective-permute-done.2
  84.6 3.8 %collective-permute-done.3 = bf16[6,20,296]{2,1,0:T(8,128)(2,1)S(1)} collective-permute-done((bf16[6,20,296]{2,1,0:T(8,128)(2,1)S(1)}, bf16[6,20,296]{2,1,0:T(8,128)(2,1)S(1)}, u32[]{:S(2)}, u32[]{:S(2)}) %collective-permute-start.3) | collective-permute-done | bytes 71072 | tf_op jit(solution)/shard_map/ppermute | solution.py:20
  88.3 0.6 pad_maximum_fusion.1
  88.9 44.0 %while.11 = (s32[]{:T(128)}, f32[6,128,256]{2,1,0:T(8,128)}, bf16[6,168,296]{2,1,0:T(8,128)(2,1)S(1)}, bf16[6,41,41]{2,1,0:T(8,128)(2,1)S(1)}, s32[296,256]{1,0:T(8,128)S(1)}, /*index=5*/s32[]{:T(128)}) while((s32[]{:T(128)}, f32[6,128,256]{2,1,0:T(8,128)}, bf16[6,168,296]{2,1,0:T(8,128)(2,1)S(1)}, ...), condition=%wide.region_5.6_spmd.clone, body=%wide.region_4.5_spmd.clone.sunk | while | flops 1309280256 | bytes 26491468 | solution.py:116
  88.9 2.2 %fusion.75 = bf16[41,296,256]{2,0,1:T(8,128)(2,1)S(1)} fusion(s32[296,256]{1,0:T(8,128)S(1)} %get-tuple-element.138, bf16[6,41,41]{2,1,0:T(8,128)(2,1)S(1)} %get-tuple-element.137, s32[]{:T(128)} %get-tuple-element.128), kind=kOutput, calls=%fused_computation.5.clone.1 | convolution fusion | flops 264079360 | bytes 6529028 | tf_op jit(solution)/shard_map/while/body/eval_jaxpr/dk,kpx->pdx/dot_general | solution.py:104
  91.1 4.0 %fusion.76 = f32[168,41,256]{2,0,1:T(8,128)S(1)} fusion(bf16[6,168,296]{2,1,0:T(8,128)(2,1)S(1)} %get-tuple-element.136, s32[]{:T(128)} %get-tuple-element.128, bf16[37,8,41,256]{3,2,1,0:T(8,128)(2,1)S(1)} %bitcast.267), kind=kOutput, calls=%fused_computation.6.clone.1 | convolution fusion | flops 1043890176 | bytes 14456836 | tf_op jit(solution)/shard_map/while/body/eval_jaxpr/dot_general | solution.py:107
  95.1 1.2 fusion.77
  96.2 2.2 %fusion.75 = bf16[41,296,256]{2,0,1:T(8,128)(2,1)S(1)} fusion(s32[296,256]{1,0:T(8,128)S(1)} %get-tuple-element.138, bf16[6,41,41]{2,1,0:T(8,128)(2,1)S(1)} %get-tuple-element.137, s32[]{:T(128)} %get-tuple-element.128), kind=kOutput, calls=%fused_computation.5.clone.1 | convolution fusion | flops 264079360 | bytes 6529028 | tf_op jit(solution)/shard_map/while/body/eval_jaxpr/dk,kpx->pdx/dot_general | solution.py:104
  98.4 4.0 %fusion.76 = f32[168,41,256]{2,0,1:T(8,128)S(1)} fusion(bf16[6,168,296]{2,1,0:T(8,128)(2,1)S(1)} %get-tuple-element.136, s32[]{:T(128)} %get-tuple-element.128, bf16[37,8,41,256]{3,2,1,0:T(8,128)(2,1)S(1)} %bitcast.267), kind=kOutput, calls=%fused_computation.6.clone.1 | convolution fusion | flops 1043890176 | bytes 14456836 | tf_op jit(solution)/shard_map/while/body/eval_jaxpr/dot_general | solution.py:107
  102.4 1.2 fusion.77
  103.6 2.2 %fusion.75 = bf16[41,296,256]{2,0,1:T(8,128)(2,1)S(1)} fusion(s32[296,256]{1,0:T(8,128)S(1)} %get-tuple-element.138, bf16[6,41,41]{2,1,0:T(8,128)(2,1)S(1)} %get-tuple-element.137, s32[]{:T(128)} %get-tuple-element.128), kind=kOutput, calls=%fused_computation.5.clone.1 | convolution fusion | flops 264079360 | bytes 6529028 | tf_op jit(solution)/shard_map/while/body/eval_jaxpr/dk,kpx->pdx/dot_general | solution.py:104
  105.8 4.0 %fusion.76 = f32[168,41,256]{2,0,1:T(8,128)S(1)} fusion(bf16[6,168,296]{2,1,0:T(8,128)(2,1)S(1)} %get-tuple-element.136, s32[]{:T(128)} %get-tuple-element.128, bf16[37,8,41,256]{3,2,1,0:T(8,128)(2,1)S(1)} %bitcast.267), kind=kOutput, calls=%fused_computation.6.clone.1 | convolution fusion | flops 1043890176 | bytes 14456836 | tf_op jit(solution)/shard_map/while/body/eval_jaxpr/dot_general | solution.py:107
  109.7 1.2 fusion.77
  110.9 2.2 %fusion.75 = bf16[41,296,256]{2,0,1:T(8,128)(2,1)S(1)} fusion(s32[296,256]{1,0:T(8,128)S(1)} %get-tuple-element.138, bf16[6,41,41]{2,1,0:T(8,128)(2,1)S(1)} %get-tuple-element.137, s32[]{:T(128)} %get-tuple-element.128), kind=kOutput, calls=%fused_computation.5.clone.1 | convolution fusion | flops 264079360 | bytes 6529028 | tf_op jit(solution)/shard_map/while/body/eval_jaxpr/dk,kpx->pdx/dot_general | solution.py:104
  113.1 4.0 %fusion.76 = f32[168,41,256]{2,0,1:T(8,128)S(1)} fusion(bf16[6,168,296]{2,1,0:T(8,128)(2,1)S(1)} %get-tuple-element.136, s32[]{:T(128)} %get-tuple-element.128, bf16[37,8,41,256]{3,2,1,0:T(8,128)(2,1)S(1)} %bitcast.267), kind=kOutput, calls=%fused_computation.6.clone.1 | convolution fusion | flops 1043890176 | bytes 14456836 | tf_op jit(solution)/shard_map/while/body/eval_jaxpr/dot_general | solution.py:107
  117.1 1.2 fusion.77
  118.2 2.2 %fusion.75 = bf16[41,296,256]{2,0,1:T(8,128)(2,1)S(1)} fusion(s32[296,256]{1,0:T(8,128)S(1)} %get-tuple-element.138, bf16[6,41,41]{2,1,0:T(8,128)(2,1)S(1)} %get-tuple-element.137, s32[]{:T(128)} %get-tuple-element.128), kind=kOutput, calls=%fused_computation.5.clone.1 | convolution fusion | flops 264079360 | bytes 6529028 | tf_op jit(solution)/shard_map/while/body/eval_jaxpr/dk,kpx->pdx/dot_general | solution.py:104
  120.4 4.0 %fusion.76 = f32[168,41,256]{2,0,1:T(8,128)S(1)} fusion(bf16[6,168,296]{2,1,0:T(8,128)(2,1)S(1)} %get-tuple-element.136, s32[]{:T(128)} %get-tuple-element.128, bf16[37,8,41,256]{3,2,1,0:T(8,128)(2,1)S(1)} %bitcast.267), kind=kOutput, calls=%fused_computation.6.clone.1 | convolution fusion | flops 1043890176 | bytes 14456836 | tf_op jit(solution)/shard_map/while/body/eval_jaxpr/dot_general | solution.py:107
  124.4 1.2 fusion.77
  125.6 2.2 %fusion.75 = bf16[41,296,256]{2,0,1:T(8,128)(2,1)S(1)} fusion(s32[296,256]{1,0:T(8,128)S(1)} %get-tuple-element.138, bf16[6,41,41]{2,1,0:T(8,128)(2,1)S(1)} %get-tuple-element.137, s32[]{:T(128)} %get-tuple-element.128), kind=kOutput, calls=%fused_computation.5.clone.1 | convolution fusion | flops 264079360 | bytes 6529028 | tf_op jit(solution)/shard_map/while/body/eval_jaxpr/dk,kpx->pdx/dot_general | solution.py:104
  127.8 4.0 %fusion.76 = f32[168,41,256]{2,0,1:T(8,128)S(1)} fusion(bf16[6,168,296]{2,1,0:T(8,128)(2,1)S(1)} %get-tuple-element.136, s32[]{:T(128)} %get-tuple-element.128, bf16[37,8,41,256]{3,2,1,0:T(8,128)(2,1)S(1)} %bitcast.267), kind=kOutput, calls=%fused_computation.6.clone.1 | convolution fusion | flops 1043890176 | bytes 14456836 | tf_op jit(solution)/shard_map/while/body/eval_jaxpr/dot_general | solution.py:107
  131.7 1.2 fusion.77
  (11 shorter events, 0.1 us)
Async XLA Ops:
  0.0 75.0 %copy-start = (f32[5,41,41]{2,1,0:T(8,128)S(1)}, f32[5,41,41]{2,1,0:T(8,128)}, u32[]{:S(2)}) copy-start(f32[5,41,41]{2,1,0:T(8,128)} %param.18) | copy-start | bytes 100864
  0.0 17.5 %copy-start.1 = (f32[128,8,256]{2,1,0:T(8,128)S(1)}, f32[128,8,256]{2,1,0:T(8,128)}, u32[]{:S(2)}) copy-start(f32[128,8,256]{2,1,0:T(8,128)} %param.11) | copy-start | bytes 3145732
  4.4 21.6 %all-to-all-start = ((s32[128,2,2]{1,2,0:T(2,128)}), s32[128,2,2]{1,2,0:T(2,128)S(1)}, u32[]{:S(2)}, u32[]{:S(2)}) async-start(s32[128,2,2]{1,2,0:T(2,128)} %copy.48), calls=%async_computation | async-start | bytes 262144 | tf_op jit(solution)/shard_map/all_to_all | solution.py:70
  23.3 9.8 %copy-start.2 = (f32[1,1,6,5]{2,1,3,0:T(1,128)S(1)}, f32[1,1,6,5]{2,1,3,0:T(1,128)}, u32[]{:S(2)}) copy-start(f32[1,1,6,5]{2,1,3,0:T(1,128)} %param.19) | copy-start | bytes 364
  26.0 36.8 %all-to-all-start.1 = ((bf16[256,8,2,256]{3,2,1,0:T(2,128)(2,1)}), bf16[256,8,2,256]{3,2,1,0:T(2,128)(2,1)S(1)}, u32[]{:S(2)}, u32[]{:S(2)}) async-start(bf16[256,8,2,256]{3,2,1,0:T(2,128)(2,1)} %reshape.559), calls=%async_computation.1 | async-start | bytes 4194304 | tf_op jit(solution)/shard_map/all_to_all | solution.py:69
  69.7 6.0 %collective-permute-start = (bf16[6,128,20]{2,1,0:T(8,128)(2,1)S(1)}, bf16[6,128,20]{2,1,0:T(8,128)(2,1)S(1)}, u32[]{:S(2)}, u32[]{:S(2)}) collective-permute-start(bf16[6,128,20]{2,1,0:T(8,128)(2,1)S(1)} %get-tuple-element.85), channel_id=1, source_target_pairs={{0,16},{16,32},{32,48},{48,64},{64,80},{80,96},{96,112},{1,17},{17... | collective-permute-start | bytes 92168 | tf_op jit(solution)/shard_map/ppermute | solution.py:17
  73.1 7.0 %collective-permute-start.1 = (bf16[6,128,20]{2,1,0:T(8,128)(2,1)S(1)}, bf16[6,128,20]{2,1,0:T(8,128)(2,1)S(1)}, u32[]{:S(2)}, u32[]{:S(2)}) collective-permute-start(bf16[6,128,20]{2,1,0:T(8,128)(2,1)S(1)} %get-tuple-element.86), channel_id=1, source_target_pairs={{16,0},{32,16},{48,32},{64,48},{80,64},{96,80},{112,96},{17,1},{33... | collective-permute-start | bytes 92168 | tf_op jit(solution)/shard_map/ppermute | solution.py:20
  80.2 4.3 %collective-permute-start.2 = (bf16[6,20,296]{2,1,0:T(8,128)(2,1)S(1)}, bf16[6,20,296]{2,1,0:T(8,128)(2,1)S(1)}, u32[]{:S(2)}, u32[]{:S(2)}) collective-permute-start(bf16[6,20,296]{2,1,0:T(8,128)(2,1)S(1)} %get-tuple-element.83), channel_id=1, source_target_pairs={{0,1},{1,2},{2,3},{3,4},{4,5},{5,6},{6,7},{7,8},{8,9},{9,10},{10,1... | collective-permute-start | bytes 213128 | tf_op jit(solution)/shard_map/ppermute | solution.py:17
  82.8 5.5 %collective-permute-start.3 = (bf16[6,20,296]{2,1,0:T(8,128)(2,1)S(1)}, bf16[6,20,296]{2,1,0:T(8,128)(2,1)S(1)}, u32[]{:S(2)}, u32[]{:S(2)}) collective-permute-start(bf16[6,20,296]{2,1,0:T(8,128)(2,1)S(1)} %get-tuple-element.84), channel_id=1, source_target_pairs={{1,0},{2,1},{3,2},{4,3},{5,4},{6,5},{7,6},{8,7},{9,8},{10,9},{11,1... | collective-permute-start | bytes 213128 | tf_op jit(solution)/shard_map/ppermute | solution.py:20
where the time goes:
time: 134 us; the launch traced here: 133 us
  matrix products  39.8 us (30%)
  waiting for transfers between devices  39.8 us (30%)
  starting transfers between devices  27.9 us (21%)
  local copies, waits for them, and re-layouts  13.3 us (10%)
  other arithmetic  11.8 us (9%)
    all_to_all x1, waiting for transfers between devices, on_device(): lax.all_to_all(send_data, ('col', 'row'), split_axis=0, concat_axis=0, ti...  28.4 us
    dot_general x6, matrix products, convolve(): jnp.dot(image, toeplitz.reshape(wide_cols, KS * patch_cols), preferred_el...  23.9 us
    dot_general x6, matrix products, convolve(): jnp.einsum('dk,kpx->pdx', taps, table, preferred_element_type=jnp.float32)  13.1 us
    all_to_all x1, starting transfers between devices, on_device(): lax.all_to_all(send_labels, ('col', 'row'), split_axis=0, concat_axis=0,...  11.5 us
    ppermute x2, waiting for transfers between devices, extended(): lax.ppermute(lax.slice_in_dim(block, 0, width, axis=dim), axis, backward)  8.16 us
    all_to_all x1, starting transfers between devices, on_device(): lax.all_to_all(send_data, ('col', 'row'), split_axis=0, concat_axis=0, ti...  7.05 us
    dynamic_update_slice x6, other arithmetic, on_device(): return lax.map(convolve, (padded, kernel))  6.94 us
    ppermute x2, starting transfers between devices, extended(): lax.ppermute(lax.slice_in_dim(block, block.shape[dim] - width, None, axis...  5.97 us
  transfers between devices with their start and end apart: 6, of which 6 were waited for; matrix products, arithmetic and copies ran while one was open for 7% of the time, Pallas kernels for 0%

commit v1 on v0

v1 whole, which is shorter than its diff:
```python
import jax
import jax.numpy as jnp
from jax import lax
from jax.experimental import pallas as pl
from jax.experimental.pallas import tpu as pltpu
from jax.sharding import PartitionSpec as P

BANDS = 6
NBASIS = 5
KS = 41
HALF = 20
PH = 128
PW = 256
BH = 8
MESH = pl.DeviceIdType.MESH

STEP_X = (-1782682714, -1921033681, 1934304481, 809635604)
STEP_Y = (1734851178, 1843253947, 483576120, 202408901)
STEP_Z = (1524231834, 502626494, -985886066, 50605265)

GROUP = 4
TILE = 64
TAPS = 48
SHIFTS = TAPS // GROUP
ROWS = PH + 64
FIRST = 32 - HALF
OUT_ROWS = 528


def iota(shape, dim):
    return lax.broadcasted_iota(jnp.int32, shape, dim)


def body(
    coef_ref,
    patch_ref,
    offset_ref,
    exposure_ref,
    band_ref,
    basis_ref,
    pix_hbm,
    ivar_hbm,
    mask_hbm,
    out_hbm,
    pix,
    ivar,
    mask,
    table,
    table_s,
    label,
    label_in,
    data,
    data_in,
    sums,
    weights,
    mean_b,
    packs,
    above,
    below,
    side_l,
    side_r,
    image32,
    image2,
    prod,
    out_v,
    in_sem,
    table_sem,
    data_send,
    data_recv,
    label_send,
    label_recv,
    halo_send,
    halo_recv,
    out_sem,
):
    col = lax.axis_index("col")
    row = lax.axis_index("row")
    me = col * 16 + row
    z, core, x, y = col >> 1, col & 1, row >> 2, row & 3

    loads = [
        pltpu.make_async_copy(src, dst, in_sem.at[i])
        for i, (src, dst) in enumerate(((pix_hbm, pix), (ivar_hbm, ivar), (mask_hbm, mask)))
    ]
    barrier = pltpu.get_barrier_semaphore()

    def greet(k, _):
        peer = (me + k) & 127
        pl.semaphore_signal(barrier, inc=1, device_id=(peer >> 4, peer & 15), device_id_type=MESH)
        return 0

    lax.fori_loop(1, 128, greet, 0)
    for load in loads:
        load.start()

    square = (128, 128)
    sub, lane = iota(square, 0), iota(square, 1)
    diag = sub == lane

    def to_column(line):
        return jnp.sum(jnp.where(diag, line, 0.0), axis=1, keepdims=True)

    def to_line(column):
        return jnp.sum(jnp.where(diag, column, 0.0), axis=0, keepdims=True)

    subf, lanef = sub.astype(jnp.float32), lane.astype(jnp.float32)
    patch = patch_ref[...].astype(jnp.float32)
    band_col = to_column(band_ref[...].astype(jnp.float32))
    band_line = jnp.sum(
        jnp.where(exposure_ref[...].astype(jnp.float32) == subf, band_col, 0.0), axis=0, keepdims=True
    )
    key_line = band_line * float(PH) + offset_ref[...].astype(jnp.float32)
    named = patch == subf
    low = jnp.min(jnp.where(named, lanef, 128.0), axis=1, keepdims=True)
    high = jnp.max(jnp.where(named, lanef, -1.0), axis=1, keepdims=True)
    key_low = jnp.sum(jnp.where(lanef == low, key_line, 0.0), axis=1, keepdims=True)
    key_high = jnp.sum(jnp.where(lanef == high, key_line, 0.0), axis=1, keepdims=True)
    key_low = jnp.where(low < 128.0, key_low, -1000.0)
    key_high = jnp.where(high > low, key_high, -1000.0)
    place = (lane & 15) < BH
    label[...] = (jnp.where(place, key_low, key_high) + (lane & 7).astype(jnp.float32)).astype(jnp.int32)
    low_line = to_line(jnp.minimum(low, 127.0))
    high_line = to_line(jnp.maximum(high, 0.0))
    table[...] = jnp.where(iota((8, 128), 0) == 0, low_line, high_line).astype(jnp.int32)
    to_smem = pltpu.make_async_copy(table, table_s, table_sem)
    to_smem.start()
    to_smem.wait()

    for load in loads:
        load.wait()
    pl.semaphore_wait(barrier, 127)

    def fill(owner, into, at):
        first, second = table_s[0, owner] & 127, table_s[1, owner] & 127
        w0 = mask[first].astype(jnp.float32) * ivar[first].astype(jnp.float32)
        w1 = mask[second].astype(jnp.float32) * ivar[second].astype(jnp.float32)
        p0, p1 = w0 * pix[first], w1 * pix[second]
        into[pl.ds(at, 16), 0:PW] = jnp.concatenate([p0, p1], axis=0).astype(jnp.bfloat16)
        into[pl.ds(at, 16), PW : 2 * PW] = jnp.concatenate([w0, w1], axis=0).astype(jnp.bfloat16)

    def transfer(k, owner, group, target):
        rows = pl.ds(pl.multiple_of(k * 16, 16), 16)
        return (
            pltpu.make_async_remote_copy(
                src_ref=data.at[rows],
                dst_ref=data_in.at[rows],
                send_sem=data_send,
                recv_sem=data_recv.at[group],
                device_id=target,
                device_id_type=MESH,
            ),
            pltpu.make_async_remote_copy(
                src_ref=label.at[pl.ds(owner, 1)],
                dst_ref=label_in.at[pl.ds(k, 1)],
                send_sem=label_send,
                recv_sem=label_recv.at[group],
                device_id=target,
                device_id_type=MESH,
            ),
        )

    for group in range(8):
        words = [steps[group >> 1] for steps in (STEP_X, STEP_Y, STEP_Z)]

        def send(m, _, group=group, words=words):
            k = group * 16 + m
            shift = ((group & 1) * 8 + (m >> 1)) * 2
            dx, dy, dz = [(jnp.int32(word) >> shift) & 3 for word in words]
            other = m & 1
            if group == 7:
                other = other ^ (m >> 3 & m >> 2 & m >> 1 & 1)
            to_col = ((z + dz) & 3) * 2 + (core ^ other)
            to_row = ((x + dx) & 3) * 4 + ((y + dy) & 3)
            owner = to_col * 16 + to_row
            fill(owner, data, pl.multiple_of(k * 16, 16))
            for copy in transfer(k, owner, group, (to_col, to_row)):
                copy.start()
            return 0

        lax.fori_loop(0, 15 if group == 7 else 16, send, 0)
    fill(me, data_in, 127 * 16)
    own = pltpu.make_async_copy(label.at[pl.ds(me, 1)], label_in.at[pl.ds(127, 1)], table_sem)
    own.start()
    own.wait()

    def build(b, _):
        taps = coef_ref[b * NBASIS] * basis_ref[0]
        for k in range(1, NBASIS):
            taps = taps + coef_ref[b * NBASIS + k] * basis_ref[k]
        for d in range(TAPS):
            i, s = d // GROUP, d % GROUP
            base = pltpu.roll(jnp.broadcast_to(taps[d : d + 1], (8, 128)), 0, 1, stride=1, stride_axis=0)
            spread = jnp.concatenate(
                [pltpu.roll(base, (128 - HALF + q) % 128, 1) for q in range(0, TILE, 8)], axis=0
            )
            weights[b, s * TILE : (s + 1) * TILE, i * 128 : (i + 1) * 128] = spread.astype(jnp.bfloat16)
        return 0

    lax.fori_loop(0, BANDS, build, 0)

    for group in range(8):
        count = 15 if group == 7 else 16
        big = pl.ds(group * 256, count * 16)
        small = pl.ds(group * 16, count)
        pltpu.make_async_remote_copy(
            src_ref=label.at[small], dst_ref=label_in.at[small], send_sem=label_send,
            recv_sem=label_recv.at[group], device_id=(col ^ 1, row), device_id_type=MESH,
        ).wait_recv()
        pltpu.make_async_remote_copy(
            src_ref=data.at[big], dst_ref=data_in.at[big], send_sem=data_send,
            recv_sem=data_recv.at[group], device_id=(col ^ 1, row), device_id_type=MESH,
        ).wait_recv()
        pick = iota((8, 128), 1) >> 4 == iota((8, 128), 0)
        lines = [
            jnp.sum(
                jnp.where(pick, label_in[group * 16 + h * 8 : group * 16 + h * 8 + 8].astype(jnp.float32), 0.0),
                axis=0,
                keepdims=True,
            )
            for h in range(2)
        ]
        line = jnp.concatenate(lines, axis=1).astype(jnp.int32)
        for b in range(BANDS):
            hit = iota((PH, 256), 0) + b * PH == line
            part = jnp.dot(
                hit.astype(jnp.float32).astype(jnp.bfloat16),
                data_in[group * 256 : (group + 1) * 256],
                preferred_element_type=jnp.float32,
            )
            if group:
                sums[b] += part
            else:
                sums[b] = part

    pltpu.make_async_remote_copy(
        src_ref=data.at[pl.ds(0, 127 * 16)], dst_ref=data_in.at[pl.ds(0, 127 * 16)], send_sem=data_send,
        recv_sem=data_recv.at[0], device_id=(col ^ 1, row), device_id_type=MESH,
    ).wait_send()
    pltpu.make_async_remote_copy(
        src_ref=label.at[pl.ds(0, 127)], dst_ref=label_in.at[pl.ds(0, 127)], send_sem=label_send,
        recv_sem=label_recv.at[0], device_id=(col ^ 1, row), device_id_type=MESH,
    ).wait_send()

    lane_p = iota((PH, 128), 1)
    pack_l = jnp.zeros((PH, 128), jnp.float32)
    pack_r = jnp.zeros((PH, 128), jnp.float32)
    for b in range(BANDS):
        mean = sums[b, :, 0:PW] / jnp.maximum(sums[b, :, PW : 2 * PW], 1.0)
        sums[b, :, 0:PW] = mean
        mean_b[b] = mean.astype(jnp.bfloat16)
        here = (lane_p >= b * HALF) & (lane_p < (b + 1) * HALF)
        pack_l = jnp.where(here, pltpu.roll(mean[:, 0:128], b * HALF, 1), pack_l)
        pack_r = jnp.where(here, pltpu.roll(mean[:, 128:256], (b * HALF + HALF) % 128, 1), pack_r)
    packs[0] = pack_l.astype(jnp.bfloat16)
    packs[1] = pack_r.astype(jnp.bfloat16)

    up, down = (row + 15) & 15, (row + 1) & 15
    left, right = (col + 7) & 7, (col + 1) & 7
    routes = (
        (mean_b.at[:, PH - 32 : PH], above, (col, down)),
        (mean_b.at[:, 0:32], below, (col, up)),
        (packs.at[0], side_r.at[32 : 32 + PH], (left, row)),
        (packs.at[1], side_l.at[32 : 32 + PH], (right, row)),
        (packs.at[0, PH - 32 : PH], side_r.at[0:32], (left, down)),
        (packs.at[1, PH - 32 : PH], side_l.at[0:32], (right, down)),
        (packs.at[0, 0:32], side_r.at[32 + PH : ROWS], (left, up)),
        (packs.at[1, 0:32], side_l.at[32 + PH : ROWS], (right, up)),
    )
    halos = [
        pltpu.make_async_remote_copy(
            src_ref=src, dst_ref=dst, send_sem=halo_send.at[i], recv_sem=halo_recv.at[i],
            device_id=target, device_id_type=MESH,
        )
        for i, (src, dst, target) in enumerate(routes)
    ]
    for halo in halos:
        halo.start()
    for halo in halos:
        halo.wait()

    lane_r = iota((ROWS, 128), 1)
    sub_r = iota((ROWS, 128), 0)
    has_up, has_down, has_left, has_right = row > 0, row < 15, col > 0, col < 7
    live = jnp.where(has_up, 0, 32), jnp.where(has_down, ROWS, ROWS - 32)
    inside = (sub_r >= live[0]) & (sub_r < live[1])
    lane_o = iota((PH, 128), 1)

    def convolve(b, _):
        top = jnp.where(has_up, above[b].astype(jnp.float32), 0.0)
        bottom = jnp.where(has_down, below[b].astype(jnp.float32), 0.0)
        full = jnp.concatenate([top, sums[b, :, 0:PW], bottom], axis=0)
        tile0, tile1 = full[:, 0:128], full[:, 128:256]
        back = 128 - b * HALF
        edge_l = pltpu.roll(side_l[...].astype(jnp.float32), (back + 108) & 127, 1)
        edge_r = pltpu.roll(side_r[...].astype(jnp.float32), back & 127, 1)
        edge_l = jnp.where(inside & has_left, edge_l, 0.0)
        edge_r = jnp.where(inside & has_right, edge_r, 0.0)
        windows = (
            jnp.where(lane_r < 108, tile0, edge_l),
            pltpu.roll(jnp.where(lane_r < 32, tile1, tile0), 64, 1),
            jnp.where(lane_r < 108, tile1, tile0),
            pltpu.roll(jnp.where(lane_r < 32, edge_r, tile1), 64, 1),
        )
        for a, window in enumerate(windows):
            image32[pl.ds(a, ROWS, stride=4), :] = window
        low = image32[0 : 4 * ROWS].astype(jnp.bfloat16)
        image2[:, 0:128] = low
        image2[0 : 4 * ROWS - 16, 128:256] = low[16:]
        left_side = jnp.concatenate(
            [image2[4 * FIRST + 32 * p : 4 * FIRST + 32 * p + OUT_ROWS] for p in range(SHIFTS // 2)], axis=1
        )
        full_prod = lax.dot_general(
            left_side, weights[b], (((1,), (1,)), ((), ())), preferred_element_type=jnp.float32
        )
        prod[0 : OUT_ROWS - 8] = full_prod[0 : OUT_ROWS - 8, 0:128] + full_prod[8:OUT_ROWS, 128:256]
        for h in range(2):
            e0 = prod[pl.ds(2 * h, PH, stride=4), :]
            e0n = prod[pl.ds(2 * h + 4, PH, stride=4), :]
            e1 = prod[pl.ds(2 * h + 1, PH, stride=4), :]
            e1n = prod[pl.ds(2 * h + 5, PH, stride=4), :]
            kept = jnp.where(lane_o < TILE, e0, e1n)
            moved = jnp.where(lane_o < TILE, e1, e0n)
            out_v[b, :, h * 128 : (h + 1) * 128] = kept + pltpu.roll(moved, TILE, 1)
        return 0

    lax.fori_loop(0, BANDS, convolve, 0)
    result = pltpu.make_async_copy(out_v, out_hbm, out_sem)
    result.start()
    result.wait()


def on_device(
    block_pixels,
    block_ivar,
    block_mask,
    block_patch,
    block_offset,
    block_exposure,
    exposure_band,
    basis,
    coefficients,
):
    f32, bf16, i32 = jnp.float32, jnp.bfloat16, jnp.int32
    lines = [block_patch.reshape(1, 128), block_offset.reshape(1, 128), block_exposure.reshape(1, 128)]
    lines.append(jnp.pad(exposure_band, (0, 128 - exposure_band.shape[0])).reshape(1, 128))
    taps = jnp.pad(basis, ((0, 0), (0, TAPS - KS), (0, 128 - KS)))
    vmem, smem, hbm = pltpu.VMEM, pltpu.SMEM, pl.ANY
    dma = pltpu.SemaphoreType.DMA
    return pl.pallas_call(
        body,
        out_shape=jax.ShapeDtypeStruct((BANDS, PH, PW), f32),
        in_specs=[pl.BlockSpec(memory_space=smem)]
        + [pl.BlockSpec(memory_space=vmem)] * 5
        + [pl.BlockSpec(memory_space=hbm)] * 3,
        out_specs=pl.BlockSpec(memory_space=hbm),
        scratch_shapes=[
            vmem((128, BH, PW), f32),
            vmem((128, BH, PW), bf16),
            vmem((128, BH, PW), i32),
            vmem((8, 128), i32),
            smem((8, 128), i32),
            vmem((128, 128), i32),
            vmem((128, 128), i32),
            vmem((2048, 2 * PW), bf16),
            vmem((2048, 2 * PW), bf16),
            vmem((BANDS, PH, 2 * PW), f32),
            vmem((BANDS, GROUP * TILE, SHIFTS * 128), bf16),
            vmem((BANDS, PH, PW), bf16),
            vmem((2, PH, 128), bf16),
            vmem((BANDS, 32, PW), bf16),
            vmem((BANDS, 32, PW), bf16),
            vmem((ROWS, 128), bf16),
            vmem((ROWS, 128), bf16),
            vmem((4 * ROWS + 8, 128), f32),
            vmem((4 * ROWS, 256), bf16),
            vmem((OUT_ROWS, 128), f32),
            vmem((BANDS, PH, PW), f32),
            dma((3,)),
            dma,
            dma,
            dma((8,)),
            dma,
            dma((8,)),
            dma((8,)),
            dma((8,)),
            dma,
        ],
        compiler_params=pltpu.CompilerParams(
            collective_id=0, has_side_effects=True, vmem_limit_bytes=48 << 20
        ),
        cost_estimate=pl.CostEstimate(flops=6 << 30, bytes_accessed=4 << 20, transcendentals=0),
    )(coefficients.reshape(BANDS * NBASIS), *lines, taps, block_pixels, block_ivar, block_mask)


def solution(mesh):
    placed = (
        P(("col", "row"), None, None),
        P(("col", "row"), None, None),
        P(("col", "row"), None, None),
        P(("col", "row"), None),
        P(("col", "row")),
        P(("col", "row")),
        P(),
        P(),
        P("row", "col", None, None),
    )
    return jax.shard_map(
        on_device, mesh=mesh, in_specs=placed, out_specs=P(None, "row", "col"), check_vma=False
    )
```

time: 134 us -> 58.7 us (0.44)
  Pallas kernels: 0 us -> 52.2 us
  matrix products: 39.8 us -> 0 us
  waiting for transfers between devices: 39.8 us -> 0 us
  starting transfers between devices: 27.9 us -> 0 us
  other arithmetic: 11.8 us -> 0 us
  local copies, waits for them, and re-layouts: 13.3 us -> 6.19 us
    pallas_call x0 -> x1, Pallas kernels: none -> 52.2 us  [on_device(): pl.pallas_call(body, out_shape=jax.ShapeDtypeStruct((BANDS, PH, PW), f32)...]
    dot_general x15 -> x0, matrix products: 39.8 us -> none  [the longest x6 23.9 us: convolve(): jnp.dot(image, toeplitz.reshape(wide_cols, KS * patch_cols), preferred_el...]
    all_to_all x2 -> x0, waiting for transfers between devices: 31.1 us -> none  [the longest x1 28.4 us: on_device(): lax.all_to_all(send_data, ('col', 'row'), split_axis=0, concat_axis=0, ti...]
    all_to_all x2 -> x0, starting transfers between devices: 18.5 us -> none  [the longest x1 11.5 us: on_device(): lax.all_to_all(send_labels, ('col', 'row'), split_axis=0, concat_axis=0,...]
    ppermute x4 -> x0, starting transfers between devices: 9.36 us -> none  [the longest x2 5.97 us: extended(): lax.ppermute(lax.slice_in_dim(block, block.shape[dim] - width, None, axis...]
    ppermute x4 -> x0, waiting for transfers between devices: 8.7 us -> none  [the longest x2 8.16 us: extended(): lax.ppermute(lax.slice_in_dim(block, 0, width, axis=dim), axis, backward)]
    dynamic_update_slice x6 -> x0, other arithmetic: 6.94 us -> none  [on_device(): return lax.map(convolve, (padded, kernel))]
    reshape x2, local copies, waits for them, and re-layouts: 5.68 us -> 0.08 us  [the longest x1 0.08 us: on_device(): coefficients.reshape(BANDS * NBASIS)]
  transfers between devices with their start and end apart: 6 -> 0, of which waited for: 6 -> 0; matrix products, arithmetic and copies ran while one was open for 7% -> 0% of each run, Pallas kernels for 0% -> 0%
where the time goes in v1:
time: 58.7 us; the launch traced here: 58.4 us
  Pallas kernels  52.2 us (89%)
  local copies, waits for them, and re-layouts  6.19 us (11%)
    pallas_call x1, Pallas kernels, on_device(): pl.pallas_call(body, out_shape=jax.ShapeDtypeStruct((BANDS, PH, PW), f32)...  52.2 us
    unnamed x18, local copies, waits for them, and re-layouts  5.15 us

profile of v1, /device:TPU:1, one launch (start us, length us, event | category | flops | bytes accessed | tf_op | source)
XLA Modules:
  0.0 58.4 jit_solution(17080754589216999454)
XLA Ops:
  0.0 0.0 copy-start.6
  0.0 0.0 copy-start.7
  0.0 0.7 %copy-done.7 = s32[96]{0:T(128)S(1)} copy-done((s32[96]{0:T(128)S(1)}, s32[96]{0:T(128)}, u32[]{:S(2)}) %copy-start.7) | copy-done | bytes 408
  0.7 0.0 copy-done.6
  0.7 0.1 copy.11
  0.8 0.1 reshape.15.coef_ref
  0.9 0.0 copy-start.3
  0.9 0.0 copy-start.4
  0.9 0.0 copy-start.5
  0.9 1.0 %pad.9.basis_ref = f32[5,48,128]{2,1,0:T(8,128)S(1)} pad(f32[5,41,41]{2,1,0:T(8,128)} %param.16, f32[]{:T(128)} %constant.3.clone.1), padding=0_0x0_7x0_87 | pad | bytes 156504 | tf_op jit(solution)/shard_map/jit(_pad)/pad | solution.py:346
  1.8 0.0 copy-done.3
  1.8 0.0 copy-done.4
  1.8 0.0 copy-done.5
  1.9 0.0 copy-start
  1.9 1.2 %copy-done = f32[128,8,256]{2,1,0:T(8,128)S(1)} copy-done((f32[128,8,256]{2,1,0:T(8,128)S(1)}, f32[128,8,256]{2,1,0:T(8,128)}, u32[]{:S(2)}) %copy-start) | copy-done | bytes 1048600
  3.1 0.0 copy-start.1
  3.1 1.2 %copy-done.1 = s32[128,8,256]{2,1,0:T(8,128)S(1)} copy-done((s32[128,8,256]{2,1,0:T(8,128)S(1)}, s32[128,8,256]{2,1,0:T(8,128)}, u32[]{:S(2)}) %copy-start.1) | copy-done | bytes 1048600
  4.3 0.0 copy-start.2
  4.3 1.0 %copy-done.2 = bf16[128,8,256]{2,1,0:T(8,128)(2,1)S(1)} copy-done((bf16[128,8,256]{2,1,0:T(8,128)(2,1)S(1)}, bf16[128,8,256]{2,1,0:T(8,128)(2,1)}, u32[]{:S(2)}) %copy-start.2) | copy-done | bytes 524312
  5.3 52.2 %shard_map.91 = f32[6,128,256]{2,1,0:T(8,128)S(1)} custom-call(f32[30]{0:T(128)S(1)} %reshape.15.coef_ref, s32[1,128]{1,0:T(1,128)S(1)} %bitcast.5, s32[1,128]{1,0:T(1,128)S(1)} %bitcast.6, s32[1,128]{1,0:T(1,128)S(1)} %bitcast.7, s32[1,128]{1,0:T(1,128)S(1)} %pad_bitcast_fusion.band_ref, f32[5,48,128]{2,1,0:T(8,128)S(1)} %pad.9.basis_ref, ...), custom_call_target="tpu_custom_call" | custom-call | flops 6442450944 | bytes 4194304 | tf_op jit(solution)/shard_map/pallas_call | solution.py:349
  57.5 0.9 %copy.13 = f32[6,128,256]{2,1,0:T(8,128)} copy(f32[6,128,256]{2,1,0:T(8,128)S(1)} %shard_map.91) | data formatting | bytes 1572864
  (1 shorter events, 0.0 us)
Async XLA Ops:
  0.0 0.7 %copy-start.6 = (f32[1,1,6,5]{2,1,3,0:T(1,128)S(1)}, f32[1,1,6,5]{2,1,3,0:T(1,128)}, u32[]{:S(2)}) copy-start(f32[1,1,6,5]{2,1,3,0:T(1,128)} %param.17) | copy-start | bytes 364
  0.0 0.7 %copy-start.7 = (s32[96]{0:T(128)S(1)}, s32[96]{0:T(128)}, u32[]{:S(2)}) copy-start(s32[96]{0:T(128)} %param.15) | copy-start | bytes 1156
  0.9 1.0 %copy-start.3 = (s32[128,1]{0,1:T(1,128)S(1)}, s32[128,1]{0,1:T(1,128)}, u32[]{:S(2)}) copy-start(s32[128,1]{0,1:T(1,128)} %param.12) | copy-start | bytes 1540
  0.9 1.0 %copy-start.4 = (s32[128]{0:T(128)S(1)}, s32[128]{0:T(128)}, u32[]{:S(2)}) copy-start(s32[128]{0:T(128)} %param.13) | copy-start | bytes 1540
  0.9 1.0 %copy-start.5 = (s32[128]{0:T(128)S(1)}, s32[128]{0:T(128)}, u32[]{:S(2)}) copy-start(s32[128]{0:T(128)} %param.14) | copy-start | bytes 1540
  1.9 1.2 %copy-start = (f32[128,8,256]{2,1,0:T(8,128)S(1)}, f32[128,8,256]{2,1,0:T(8,128)}, u32[]{:S(2)}) copy-start(f32[128,8,256]{2,1,0:T(8,128)} %pix_hbm.1) | copy-start | bytes 3145732
  3.1 1.2 %copy-start.1 = (s32[128,8,256]{2,1,0:T(8,128)S(1)}, s32[128,8,256]{2,1,0:T(8,128)}, u32[]{:S(2)}) copy-start(s32[128,8,256]{2,1,0:T(8,128)} %mask_hbm.1) | copy-start | bytes 3145732
  4.3 1.0 %copy-start.2 = (bf16[128,8,256]{2,1,0:T(8,128)(2,1)S(1)}, bf16[128,8,256]{2,1,0:T(8,128)(2,1)}, u32[]{:S(2)}) copy-start(bf16[128,8,256]{2,1,0:T(8,128)(2,1)} %ivar_hbm.1) | copy-start | bytes 1572868

commit v2 on v1

--- a/solution.py
+++ b/solution.py
@@ -32,19 +32,26 @@
 
 
 def body(
-    coef_ref,
+    pix_hbm,
+    ivar_hbm,
+    mask_hbm,
+    patch_hbm,
+    offset_hbm,
+    exposure_hbm,
+    band_hbm,
+    basis_hbm,
+    coef_hbm,
+    out_hbm,
+    pix,
+    ivar,
+    mask,
     patch_ref,
     offset_ref,
     exposure_ref,
     band_ref,
     basis_ref,
-    pix_hbm,
-    ivar_hbm,
-    mask_hbm,
-    out_hbm,
-    pix,
-    ivar,
-    mask,
+    coef_ref,
+    taps_ref,
     table,
     table_s,
     label,
@@ -80,7 +87,19 @@
 
     loads = [
         pltpu.make_async_copy(src, dst, in_sem.at[i])
-        for i, (src, dst) in enumerate(((pix_hbm, pix), (ivar_hbm, ivar), (mask_hbm, mask)))
+        for i, (src, dst) in enumerate(
+            (
+                (patch_hbm, patch_ref),
+                (offset_hbm, offset_ref),
+                (exposure_hbm, exposure_ref),
+                (band_hbm, band_ref),
+                (pix_hbm, pix),
+                (ivar_hbm, ivar),
+                (mask_hbm, mask),
+                (basis_hbm, basis_ref),
+                (coef_hbm, coef_ref),
+            )
+        )
     ]
     barrier = pltpu.get_barrier_semaphore()
 
@@ -92,6 +111,8 @@
     lax.fori_loop(1, 128, greet, 0)
     for load in loads:
         load.start()
+    for load in loads[:4]:
+        load.wait()
 
     square = (128, 128)
     sub, lane = iota(square, 0), iota(square, 1)
@@ -105,9 +126,13 @@
 
     subf, lanef = sub.astype(jnp.float32), lane.astype(jnp.float32)
     patch = patch_ref[...].astype(jnp.float32)
-    band_col = to_column(band_ref[...].astype(jnp.float32))
+    exposures = band_ref.shape[1]
+    band_line = jnp.broadcast_to(band_ref[...].astype(jnp.float32), (exposures, exposures))
+    band_col = jnp.sum(
+        jnp.where(iota(band_line.shape, 0) == iota(band_line.shape, 1), band_line, 0.0), axis=1, keepdims=True
+    )
     band_line = jnp.sum(
-        jnp.where(exposure_ref[...].astype(jnp.float32) == subf, band_col, 0.0), axis=0, keepdims=True
+        jnp.where(exposure_ref[...].astype(jnp.float32) == subf[0:exposures], band_col, 0.0), axis=0, keepdims=True
     )
     key_line = band_line * float(PH) + offset_ref[...].astype(jnp.float32)
     named = patch == subf
@@ -126,7 +151,7 @@
     to_smem.start()
     to_smem.wait()
 
-    for load in loads:
+    for load in loads[4:]:
         load.wait()
     pl.semaphore_wait(barrier, 127)
 
@@ -183,10 +208,14 @@
     own.start()
     own.wait()
 
+    taps_ref[...] = jnp.zeros_like(taps_ref)
+
     def build(b, _):
-        taps = coef_ref[b * NBASIS] * basis_ref[0]
+        combined = coef_ref[0, 0, 0, b] * basis_ref[0]
         for k in range(1, NBASIS):
-            taps = taps + coef_ref[b * NBASIS + k] * basis_ref[k]
+            combined = combined + coef_ref[0, k, 0, b] * basis_ref[k]
+        taps_ref[0:KS, 0:KS] = combined
+        taps = taps_ref[...]
         for d in range(TAPS):
             i, s = d // GROUP, d % GROUP
             base = pltpu.roll(jnp.broadcast_to(taps[d : d + 1], (8, 128)), 0, 1, stride=1, stride_axis=0)
@@ -341,22 +370,26 @@
     coefficients,
 ):
     f32, bf16, i32 = jnp.float32, jnp.bfloat16, jnp.int32
-    lines = [block_patch.reshape(1, 128), block_offset.reshape(1, 128), block_exposure.reshape(1, 128)]
-    lines.append(jnp.pad(exposure_band, (0, 128 - exposure_band.shape[0])).reshape(1, 128))
-    taps = jnp.pad(basis, ((0, 0), (0, TAPS - KS), (0, 128 - KS)))
-    vmem, smem, hbm = pltpu.VMEM, pltpu.SMEM, pl.ANY
+    lines = [v.reshape(1, v.size) for v in (block_patch, block_offset, block_exposure, exposure_band)]
+    scales = coefficients.transpose(0, 3, 1, 2)
+    vmem, smem, hbm = pltpu.VMEM, pltpu.SMEM, pltpu.HBM
     dma = pltpu.SemaphoreType.DMA
     return pl.pallas_call(
         body,
         out_shape=jax.ShapeDtypeStruct((BANDS, PH, PW), f32),
-        in_specs=[pl.BlockSpec(memory_space=smem)]
-        + [pl.BlockSpec(memory_space=vmem)] * 5
-        + [pl.BlockSpec(memory_space=hbm)] * 3,
+        in_specs=[pl.BlockSpec(memory_space=hbm)] * 9,
         out_specs=pl.BlockSpec(memory_space=hbm),
         scratch_shapes=[
             vmem((128, BH, PW), f32),
             vmem((128, BH, PW), bf16),
             vmem((128, BH, PW), i32),
+            vmem((1, 128), i32),
+            vmem((1, 128), i32),
+            vmem((1, 128), i32),
+            vmem((1, exposure_band.size), i32),
+            vmem(basis.shape, f32),
+            smem(scales.shape, f32),
+            vmem((TAPS, 128), f32),
             vmem((8, 128), i32),
             smem((8, 128), i32),
             vmem((128, 128), i32),
@@ -375,7 +408,7 @@
             vmem((4 * ROWS, 256), bf16),
             vmem((OUT_ROWS, 128), f32),
             vmem((BANDS, PH, PW), f32),
-            dma((3,)),
+            dma((9,)),
             dma,
             dma,
             dma((8,)),
@@ -386,10 +419,10 @@
             dma,
         ],
         compiler_params=pltpu.CompilerParams(
-            collective_id=0, has_side_effects=True, vmem_limit_bytes=48 << 20
+            collective_id=0, has_side_effects=True, vmem_limit_bytes=56 << 20
         ),
         cost_estimate=pl.CostEstimate(flops=6 << 30, bytes_accessed=4 << 20, transcendentals=0),
-    )(coefficients.reshape(BANDS * NBASIS), *lines, taps, block_pixels, block_ivar, block_mask)
+    )(block_pixels, block_ivar, block_mask, *lines, basis, scales)
 
 
 def solution(mesh):

time: 58.7 us -> 54.7 us (0.932)
  local copies, waits for them, and re-layouts: 6.19 us -> 2.1 us
    unnamed x18 -> x1, local copies, waits for them, and re-layouts: 5.15 us -> 2.1 us
    pad x1 -> x0, local copies, waits for them, and re-layouts: 0.95 us -> none  [on_device(): taps = jnp.pad(basis, ((0, 0), (0, TAPS - KS), (0, 128 - KS)))]
where the time goes in v2:
time: 54.7 us; the launch traced here: 54.5 us
  Pallas kernels  52.4 us (96%)
  local copies, waits for them, and re-layouts  2.1 us (4%)
    pallas_call x1, Pallas kernels, on_device(): pl.pallas_call(body, out_shape=jax.ShapeDtypeStruct((BANDS, PH, PW), f32)...  52.4 us
    unnamed x1, local copies, waits for them, and re-layouts  2.1 us

profile of v2, /device:TPU:1, one launch (start us, length us, event | category | flops | bytes accessed | tf_op | source)
XLA Modules:
  0.0 54.5 jit_solution(18277483394243055009)
XLA Ops:
  0.0 52.4 %shard_map.91 = f32[6,128,256]{2,1,0:T(8,128)} custom-call(f32[128,8,256]{2,1,0:T(8,128)} %pix_hbm.1, bf16[128,8,256]{2,1,0:T(8,128)(2,1)} %ivar_hbm.1, s32[128,8,256]{2,1,0:T(8,128)} %mask_hbm.1, s32[1,128]{1,0:T(1,128)} %bitcast.6, s32[1,128]{1,0:T(1,128)} %bitcast.7, s32[1,128]{1,0:T(1,128)} %bitcast.8, s32[1,96]{1,0:T(1,128)} %bitcast.9, ...), custom_call_target="tpu_custom_call" | custom-call | flops 6442450944 | bytes 4194304 | tf_op jit(solution)/shard_map/pallas_call | solution.py:377
  52.4 2.1 %copy.11 = f32[6,128,256]{2,1,0:T(8,128)} copy(f32[6,128,256]{2,1,0:T(8,128)} %shard_map.91) | data formatting | bytes 1572864

commit v3 on v2

--- a/solution.py
+++ b/solution.py
@@ -14,9 +14,11 @@
 BH = 8
 MESH = pl.DeviceIdType.MESH
 
-STEP_X = (-1782682714, -1921033681, 1934304481, 809635604)
-STEP_Y = (1734851178, 1843253947, 483576120, 202408901)
-STEP_Z = (1524231834, 502626494, -985886066, 50605265)
+STEP_X = (-2134884224, -1862789622, 1547504322, -997211824, 1521461850, -1521111046, -2790657, 930528599)
+STEP_Y = (-1473245152, 621707680, 130240700, 824245269, -1347790166, 1516198495, 2105372591, 904625533)
+STEP_Z = (672072970, 1252255834, -246087895, 998725, -84236886, 1437267365, -715665414, 15743)
+STEP_C = (285475844, 71372868, 1091585041, 1431572740, 1145324612, 1145324612, 286331972, 357912849)
+LINES, PLANES = 13, 64
 
 GROUP = 4
 TILE = 64
@@ -79,6 +81,8 @@
     halo_send,
     halo_recv,
     out_sem,
+    line_sem,
+    plane_sem,
 ):
     col = lax.axis_index("col")
     row = lax.axis_index("row")
@@ -102,13 +106,13 @@
         )
     ]
     barrier = pltpu.get_barrier_semaphore()
-
-    def greet(k, _):
-        peer = (me + k) & 127
-        pl.semaphore_signal(barrier, inc=1, device_id=(peer >> 4, peer & 15), device_id_type=MESH)
-        return 0
-
-    lax.fori_loop(1, 128, greet, 0)
+    on_line = (
+        [((col + d) & 7, row) for d in range(1, 8)]
+        + [(col, x * 4 + ((y + d) & 3)) for d in range(1, 4)]
+        + [(col, ((x + d) & 3) * 4 + y) for d in range(1, 4)]
+    )
+    for peer in on_line:
+        pl.semaphore_signal(barrier, inc=1, device_id=peer, device_id_type=MESH)
     for load in loads:
         load.start()
     for load in loads[:4]:
@@ -153,7 +157,6 @@
 
     for load in loads[4:]:
         load.wait()
-    pl.semaphore_wait(barrier, 127)
 
     def fill(owner, into, at):
         first, second = table_s[0, owner] & 127, table_s[1, owner] & 127
@@ -184,17 +187,14 @@
             ),
         )
 
-    for group in range(8):
-        words = [steps[group >> 1] for steps in (STEP_X, STEP_Y, STEP_Z)]
-
-        def send(m, _, group=group, words=words):
+    def send_some(first, last):
+        group = first // 16
+        words = [steps[group] for steps in (STEP_X, STEP_Y, STEP_Z, STEP_C)]
+
+        def send(m, _):
             k = group * 16 + m
-            shift = ((group & 1) * 8 + (m >> 1)) * 2
-            dx, dy, dz = [(jnp.int32(word) >> shift) & 3 for word in words]
-            other = m & 1
-            if group == 7:
-                other = other ^ (m >> 3 & m >> 2 & m >> 1 & 1)
-            to_col = ((z + dz) & 3) * 2 + (core ^ other)
+            dx, dy, dz, dc = [(jnp.int32(word) >> (2 * m)) & 3 for word in words]
+            to_col = ((z + dz) & 3) * 2 + (core ^ dc)
             to_row = ((x + dx) & 3) * 4 + ((y + dy) & 3)
             owner = to_col * 16 + to_row
             fill(owner, data, pl.multiple_of(k * 16, 16))
@@ -202,7 +202,21 @@
                 copy.start()
             return 0
 
-        lax.fori_loop(0, 15 if group == 7 else 16, send, 0)
+        lax.fori_loop(first - group * 16, last - group * 16, send, 0)
+
+    pl.semaphore_wait(barrier, len(on_line))
+    for peer in on_line:
+        pl.semaphore_signal(line_sem, inc=1, device_id=peer, device_id_type=MESH)
+    send_some(0, LINES)
+    pl.semaphore_wait(line_sem, len(on_line))
+    for peer in on_line[-3:]:
+        pl.semaphore_signal(plane_sem, inc=1, device_id=peer, device_id_type=MESH)
+    send_some(LINES, 16)
+    for first in range(16, PLANES, 16):
+        send_some(first, first + 16)
+    pl.semaphore_wait(plane_sem, 3)
+    for first in range(PLANES, 128, 16):
+        send_some(first, min(first + 16, 127))
     fill(me, data_in, 127 * 16)
     own = pltpu.make_async_copy(label.at[pl.ds(me, 1)], label_in.at[pl.ds(127, 1)], table_sem)
     own.start()
@@ -331,28 +345,29 @@
             pltpu.roll(jnp.where(lane_r < 32, edge_r, tile1), 64, 1),
         )
         for a, window in enumerate(windows):
-            image32[pl.ds(a, ROWS, stride=4), :] = window
-        low = image32[0 : 4 * ROWS].astype(jnp.bfloat16)
-        image2[:, 0:128] = low
-        image2[0 : 4 * ROWS - 16, 128:256] = low[16:]
+            image32[b & 1, pl.ds(a, ROWS, stride=4), :] = window
+        low = image32[b & 1, 0 : 4 * ROWS].astype(jnp.bfloat16)
+        image2[b & 1, :, 0:128] = low
+        image2[b & 1, 0 : 4 * ROWS - 16, 128:256] = low[16:]
         left_side = jnp.concatenate(
-            [image2[4 * FIRST + 32 * p : 4 * FIRST + 32 * p + OUT_ROWS] for p in range(SHIFTS // 2)], axis=1
+            [image2[b & 1, 4 * FIRST + 32 * p : 4 * FIRST + 32 * p + OUT_ROWS] for p in range(SHIFTS // 2)], axis=1
         )
         full_prod = lax.dot_general(
             left_side, weights[b], (((1,), (1,)), ((), ())), preferred_element_type=jnp.float32
         )
-        prod[0 : OUT_ROWS - 8] = full_prod[0 : OUT_ROWS - 8, 0:128] + full_prod[8:OUT_ROWS, 128:256]
+        prod[b & 1, 0 : OUT_ROWS - 8] = full_prod[0 : OUT_ROWS - 8, 0:128] + full_prod[8:OUT_ROWS, 128:256]
         for h in range(2):
-            e0 = prod[pl.ds(2 * h, PH, stride=4), :]
-            e0n = prod[pl.ds(2 * h + 4, PH, stride=4), :]
-            e1 = prod[pl.ds(2 * h + 1, PH, stride=4), :]
-            e1n = prod[pl.ds(2 * h + 5, PH, stride=4), :]
+            e0 = prod[b & 1, pl.ds(2 * h, PH, stride=4), :]
+            e0n = prod[b & 1, pl.ds(2 * h + 4, PH, stride=4), :]
+            e1 = prod[b & 1, pl.ds(2 * h + 1, PH, stride=4), :]
+            e1n = prod[b & 1, pl.ds(2 * h + 5, PH, stride=4), :]
             kept = jnp.where(lane_o < TILE, e0, e1n)
             moved = jnp.where(lane_o < TILE, e1, e0n)
             out_v[b, :, h * 128 : (h + 1) * 128] = kept + pltpu.roll(moved, TILE, 1)
         return 0
 
-    lax.fori_loop(0, BANDS, convolve, 0)
+    for b in range(BANDS):
+        convolve(b, 0)
     result = pltpu.make_async_copy(out_v, out_hbm, out_sem)
     result.start()
     result.wait()
@@ -404,9 +419,9 @@
             vmem((BANDS, 32, PW), bf16),
             vmem((ROWS, 128), bf16),
             vmem((ROWS, 128), bf16),
-            vmem((4 * ROWS + 8, 128), f32),
-            vmem((4 * ROWS, 256), bf16),
-            vmem((OUT_ROWS, 128), f32),
+            vmem((2, 4 * ROWS + 8, 128), f32),
+            vmem((2, 4 * ROWS, 256), bf16),
+            vmem((2, OUT_ROWS, 128), f32),
             vmem((BANDS, PH, PW), f32),
             dma((9,)),
             dma,
@@ -417,6 +432,8 @@
             dma((8,)),
             dma((8,)),
             dma,
+            pltpu.SemaphoreType.REGULAR,
+            pltpu.SemaphoreType.REGULAR,
         ],
         compiler_params=pltpu.CompilerParams(
             collective_id=0, has_side_effects=True, vmem_limit_bytes=56 << 20

time: 54.7 us -> 49.9 us (0.912)
  Pallas kernels: 52.4 us -> 47.2 us
    pallas_call x1, Pallas kernels: 52.4 us -> 47.2 us  [on_device(): pl.pallas_call(body, out_shape=jax.ShapeDtypeStruct((BANDS, PH, PW), f32)...]
where the time goes in v3:
time: 49.9 us; the launch traced here: 49.3 us
  Pallas kernels  47.2 us (95%)
  local copies, waits for them, and re-layouts  2.1 us (4%)
    pallas_call x1, Pallas kernels, on_device(): pl.pallas_call(body, out_shape=jax.ShapeDtypeStruct((BANDS, PH, PW), f32)...  47.2 us
    unnamed x1, local copies, waits for them, and re-layouts  2.1 us

profile of v3, /device:TPU:1, one launch (start us, length us, event | category | flops | bytes accessed | tf_op | source)
XLA Modules:
  0.0 49.3 jit_solution(15880769663201362817)
XLA Ops:
  0.0 47.2 %shard_map.91 = f32[6,128,256]{2,1,0:T(8,128)} custom-call(f32[128,8,256]{2,1,0:T(8,128)} %pix_hbm.1, bf16[128,8,256]{2,1,0:T(8,128)(2,1)} %ivar_hbm.1, s32[128,8,256]{2,1,0:T(8,128)} %mask_hbm.1, s32[1,128]{1,0:T(1,128)} %bitcast.6, s32[1,128]{1,0:T(1,128)} %bitcast.7, s32[1,128]{1,0:T(1,128)} %bitcast.8, s32[1,96]{1,0:T(1,128)} %bitcast.9, ...), custom_call_target="tpu_custom_call" | custom-call | flops 6442450944 | bytes 4194304 | tf_op jit(solution)/shard_map/pallas_call | solution.py:392
  47.2 2.1 %copy.11 = f32[6,128,256]{2,1,0:T(8,128)} copy(f32[6,128,256]{2,1,0:T(8,128)} %shard_map.91) | data formatting | bytes 1572864

commit v4 on v3

--- a/solution.py
+++ b/solution.py
@@ -22,7 +22,7 @@
 
 GROUP = 4
 TILE = 64
-TAPS = 48
+TAPS = 44
 SHIFTS = TAPS // GROUP
 ROWS = PH + 64
 FIRST = 32 - HALF
@@ -43,7 +43,7 @@
     band_hbm,
     basis_hbm,
     coef_hbm,
-    out_hbm,
+    out_ref,
     pix,
     ivar,
     mask,
@@ -70,8 +70,8 @@
     side_r,
     image32,
     image2,
+    full,
     prod,
-    out_v,
     in_sem,
     table_sem,
     data_send,
@@ -80,7 +80,6 @@
     label_recv,
     halo_send,
     halo_recv,
-    out_sem,
     line_sem,
     plane_sem,
 ):
@@ -284,6 +283,15 @@
         recv_sem=label_recv.at[0], device_id=(col ^ 1, row), device_id_type=MESH,
     ).wait_send()
 
+    up, down = (row + 15) & 15, (row + 1) & 15
+    left, right = (col + 7) & 7, (col + 1) & 7
+
+    def halo(src, dst, i, target):
+        return pltpu.make_async_remote_copy(
+            src_ref=src, dst_ref=dst, send_sem=halo_send.at[i], recv_sem=halo_recv.at[i],
+            device_id=target, device_id_type=MESH,
+        )
+
     lane_p = iota((PH, 128), 1)
     pack_l = jnp.zeros((PH, 128), jnp.float32)
     pack_r = jnp.zeros((PH, 128), jnp.float32)
@@ -291,86 +299,110 @@
         mean = sums[b, :, 0:PW] / jnp.maximum(sums[b, :, PW : 2 * PW], 1.0)
         sums[b, :, 0:PW] = mean
         mean_b[b] = mean.astype(jnp.bfloat16)
+        halo(mean_b.at[b, PH - 32 : PH], above.at[b], 0, (col, down)).start()
+        halo(mean_b.at[b, 0:32], below.at[b], 1, (col, up)).start()
         here = (lane_p >= b * HALF) & (lane_p < (b + 1) * HALF)
         pack_l = jnp.where(here, pltpu.roll(mean[:, 0:128], b * HALF, 1), pack_l)
         pack_r = jnp.where(here, pltpu.roll(mean[:, 128:256], (b * HALF + HALF) % 128, 1), pack_r)
     packs[0] = pack_l.astype(jnp.bfloat16)
     packs[1] = pack_r.astype(jnp.bfloat16)
-
-    up, down = (row + 15) & 15, (row + 1) & 15
-    left, right = (col + 7) & 7, (col + 1) & 7
-    routes = (
-        (mean_b.at[:, PH - 32 : PH], above, (col, down)),
-        (mean_b.at[:, 0:32], below, (col, up)),
-        (packs.at[0], side_r.at[32 : 32 + PH], (left, row)),
-        (packs.at[1], side_l.at[32 : 32 + PH], (right, row)),
-        (packs.at[0, PH - 32 : PH], side_r.at[0:32], (left, down)),
-        (packs.at[1, PH - 32 : PH], side_l.at[0:32], (right, down)),
-        (packs.at[0, 0:32], side_r.at[32 + PH : ROWS], (left, up)),
-        (packs.at[1, 0:32], side_l.at[32 + PH : ROWS], (right, up)),
-    )
-    halos = [
-        pltpu.make_async_remote_copy(
-            src_ref=src, dst_ref=dst, send_sem=halo_send.at[i], recv_sem=halo_recv.at[i],
-            device_id=target, device_id_type=MESH,
+    sides = [
+        halo(packs.at[0], side_r.at[32 : 32 + PH], 2, (left, row)),
+        halo(packs.at[1], side_l.at[32 : 32 + PH], 3, (right, row)),
+    ]
+    corners = [
+        halo(packs.at[0, PH - 32 : PH], side_r.at[0:32], 4, (left, down)),
+        halo(packs.at[1, PH - 32 : PH], side_l.at[0:32], 5, (right, down)),
+        halo(packs.at[0, 0:32], side_r.at[32 + PH : ROWS], 6, (left, up)),
+        halo(packs.at[1, 0:32], side_l.at[32 + PH : ROWS], 7, (right, up)),
+    ]
+    for copy in sides + corners:
+        copy.start()
+
+    has_up, has_down, has_left, has_right = row > 0, row < 15, col > 0, col < 7
+
+    def inner_windows(b, tile0, tile1, first):
+        rows = tile0.shape[0]
+        lanes = iota((rows, 128), 1)
+        image32[b, pl.ds(4 * first + 1, rows, stride=4), :] = pltpu.roll(jnp.where(lanes < 32, tile1, tile0), 64, 1)
+        image32[b, pl.ds(4 * first + 2, rows, stride=4), :] = jnp.where(lanes < 108, tile1, tile0)
+
+    def outer_windows(b, tile0, tile1, edge_l, edge_r, first):
+        rows = tile0.shape[0]
+        lanes = iota((rows, 128), 1)
+        edge_l = jnp.where(has_left, pltpu.roll(edge_l.astype(jnp.float32), (236 - b * HALF) % 128, 1), 0.0)
+        edge_r = jnp.where(has_right, pltpu.roll(edge_r.astype(jnp.float32), (128 - b * HALF) % 128, 1), 0.0)
+        image32[b, pl.ds(4 * first, rows, stride=4), :] = jnp.where(lanes < 108, tile0, edge_l)
+        image32[b, pl.ds(4 * first + 3, rows, stride=4), :] = pltpu.roll(jnp.where(lanes < 32, edge_r, tile1), 64, 1)
+
+    def widen(b, first, last, first2, last2):
+        image2[b, first:last, 0:128] = image32[b, first:last].astype(jnp.bfloat16)
+        image2[b, first2:last2, 128:256] = image32[b, first2 + 16 : last2 + 16].astype(jnp.bfloat16)
+
+    def matmul(b, spans):
+        pairs = [
+            jnp.concatenate(
+                [image2[b, 4 * FIRST + 32 * p + lo : 4 * FIRST + 32 * p + hi] for lo, hi in spans], axis=0
+            )
+            for p in range(SHIFTS // 2)
+        ]
+        if SHIFTS % 2:
+            pairs.append(
+                jnp.concatenate(
+                    [
+                        image2[b, 4 * FIRST + 16 * (SHIFTS - 1) + lo : 4 * FIRST + 16 * (SHIFTS - 1) + hi, 0:128]
+                        for lo, hi in spans
+                    ],
+                    axis=0,
+                )
+            )
+        result = lax.dot_general(
+            jnp.concatenate(pairs, axis=1), weights[b], (((1,), (1,)), ((), ())), preferred_element_type=jnp.float32
         )
-        for i, (src, dst, target) in enumerate(routes)
-    ]
-    for halo in halos:
-        halo.start()
-    for halo in halos:
-        halo.wait()
-
-    lane_r = iota((ROWS, 128), 1)
-    sub_r = iota((ROWS, 128), 0)
-    has_up, has_down, has_left, has_right = row > 0, row < 15, col > 0, col < 7
-    live = jnp.where(has_up, 0, 32), jnp.where(has_down, ROWS, ROWS - 32)
-    inside = (sub_r >= live[0]) & (sub_r < live[1])
-    lane_o = iota((PH, 128), 1)
-
-    def convolve(b, _):
-        top = jnp.where(has_up, above[b].astype(jnp.float32), 0.0)
-        bottom = jnp.where(has_down, below[b].astype(jnp.float32), 0.0)
-        full = jnp.concatenate([top, sums[b, :, 0:PW], bottom], axis=0)
-        tile0, tile1 = full[:, 0:128], full[:, 128:256]
-        back = 128 - b * HALF
-        edge_l = pltpu.roll(side_l[...].astype(jnp.float32), (back + 108) & 127, 1)
-        edge_r = pltpu.roll(side_r[...].astype(jnp.float32), back & 127, 1)
-        edge_l = jnp.where(inside & has_left, edge_l, 0.0)
-        edge_r = jnp.where(inside & has_right, edge_r, 0.0)
-        windows = (
-            jnp.where(lane_r < 108, tile0, edge_l),
-            pltpu.roll(jnp.where(lane_r < 32, tile1, tile0), 64, 1),
-            jnp.where(lane_r < 108, tile1, tile0),
-            pltpu.roll(jnp.where(lane_r < 32, edge_r, tile1), 64, 1),
+        at = 0
+        for lo, hi in spans:
+            full[b, lo:hi] = result[at : at + hi - lo]
+            at += hi - lo
+
+    def finish(b, lo, hi):
+        first, last = 4 * lo, 4 * hi + 8
+        prod[b, first:last] = full[b, first:last, 0:128] + full[b, first + 8 : last + 8, 128:256]
+        rows = hi - lo
+        lanes = iota((rows, 128), 1)
+        for h in range(2):
+            e0, e0n, e1, e1n = [prod[b, pl.ds(first + 2 * h + i, rows, stride=4), :] for i in (0, 4, 1, 5)]
+            kept = jnp.where(lanes < TILE, e0, e1n)
+            moved = jnp.where(lanes < TILE, e1, e0n)
+            out_ref[b, lo:hi, h * 128 : (h + 1) * 128] = kept + pltpu.roll(moved, TILE, 1)
+
+    for b in range(BANDS):
+        inner_windows(b, sums[b, :, 0:128], sums[b, :, 128:256], 32)
+    for copy in sides:
+        copy.wait()
+    for b in range(BANDS):
+        outer_windows(
+            b, sums[b, :, 0:128], sums[b, :, 128:256], side_l[32 : 32 + PH], side_r[32 : 32 + PH], 32
         )
-        for a, window in enumerate(windows):
-            image32[b & 1, pl.ds(a, ROWS, stride=4), :] = window
-        low = image32[b & 1, 0 : 4 * ROWS].astype(jnp.bfloat16)
-        image2[b & 1, :, 0:128] = low
-        image2[b & 1, 0 : 4 * ROWS - 16, 128:256] = low[16:]
-        left_side = jnp.concatenate(
-            [image2[b & 1, 4 * FIRST + 32 * p : 4 * FIRST + 32 * p + OUT_ROWS] for p in range(SHIFTS // 2)], axis=1
-        )
-        full_prod = lax.dot_general(
-            left_side, weights[b], (((1,), (1,)), ((), ())), preferred_element_type=jnp.float32
-        )
-        prod[b & 1, 0 : OUT_ROWS - 8] = full_prod[0 : OUT_ROWS - 8, 0:128] + full_prod[8:OUT_ROWS, 128:256]
-        for h in range(2):
-            e0 = prod[b & 1, pl.ds(2 * h, PH, stride=4), :]
-            e0n = prod[b & 1, pl.ds(2 * h + 4, PH, stride=4), :]
-            e1 = prod[b & 1, pl.ds(2 * h + 1, PH, stride=4), :]
-            e1n = prod[b & 1, pl.ds(2 * h + 5, PH, stride=4), :]
-            kept = jnp.where(lane_o < TILE, e0, e1n)
-            moved = jnp.where(lane_o < TILE, e1, e0n)
-            out_v[b, :, h * 128 : (h + 1) * 128] = kept + pltpu.roll(moved, TILE, 1)
-        return 0
-
+        widen(b, 128, 640, 128, 608)
+        matmul(b, ((80, 432),))
+        finish(b, 24, 104)
+
+    for copy in corners:
+        copy.wait()
+    halo(mean_b.at[:, PH - 32 : PH], above, 0, (col, down)).wait()
+    halo(mean_b.at[:, 0:32], below, 1, (col, up)).wait()
     for b in range(BANDS):
-        convolve(b, 0)
-    result = pltpu.make_async_copy(out_v, out_hbm, out_sem)
-    result.start()
-    result.wait()
+        for ref, here, first, side in ((above, has_up, 0, 0), (below, has_down, 32 + PH, 32 + PH)):
+            rows = jnp.where(here, ref[b].astype(jnp.float32), 0.0)
+            edge_l = jnp.where(here, side_l[side : side + 32].astype(jnp.float32), 0.0)
+            edge_r = jnp.where(here, side_r[side : side + 32].astype(jnp.float32), 0.0)
+            inner_windows(b, rows[:, 0:128], rows[:, 128:256], first)
+            outer_windows(b, rows[:, 0:128], rows[:, 128:256], edge_l, edge_r, first)
+        widen(b, 48, 128, 48, 128)
+        widen(b, 640, 736, 608, 736)
+        matmul(b, ((0, 80), (432, OUT_ROWS)))
+        finish(b, 0, 24)
+        finish(b, 104, 128)
 
 
 def on_device(
@@ -391,9 +423,9 @@
     dma = pltpu.SemaphoreType.DMA
     return pl.pallas_call(
         body,
-        out_shape=jax.ShapeDtypeStruct((BANDS, PH, PW), f32),
+        out_shape=vmem((BANDS, PH, PW), f32),
         in_specs=[pl.BlockSpec(memory_space=hbm)] * 9,
-        out_specs=pl.BlockSpec(memory_space=hbm),
+        out_specs=pl.BlockSpec(memory_space=vmem),
         scratch_shapes=[
             vmem((128, BH, PW), f32),
             vmem((128, BH, PW), bf16),
@@ -419,10 +451,10 @@
             vmem((BANDS, 32, PW), bf16),
             vmem((ROWS, 128), bf16),
             vmem((ROWS, 128), bf16),
-            vmem((2, 4 * ROWS + 8, 128), f32),
-            vmem((2, 4 * ROWS, 256), bf16),
-            vmem((2, OUT_ROWS, 128), f32),
-            vmem((BANDS, PH, PW), f32),
+            vmem((BANDS, 4 * ROWS + 8, 128), f32),
+            vmem((BANDS, 4 * ROWS, 256), bf16),
+            vmem((BANDS, OUT_ROWS, 256), f32),
+            vmem((BANDS, OUT_ROWS, 128), f32),
             dma((9,)),
             dma,
             dma,
@@ -431,7 +463,6 @@
             dma((8,)),
             dma((8,)),
             dma((8,)),
-            dma,
             pltpu.SemaphoreType.REGULAR,
             pltpu.SemaphoreType.REGULAR,
         ],

time: 49.9 us -> 46.2 us (0.926)
  Pallas kernels: 47.2 us -> 44.8 us
  local copies, waits for them, and re-layouts: 2.1 us -> 0.88 us
    pallas_call x1, Pallas kernels: 47.2 us -> 44.8 us  [on_device(): pl.pallas_call(body, out_shape=vmem((BANDS, PH, PW), f32), in_specs=[pl.B...]
    unnamed x1, local copies, waits for them, and re-layouts: 2.1 us -> 0.88 us
where the time goes in v4:
time: 46.2 us; the launch traced here: 45.7 us
  Pallas kernels  44.8 us (97%)
  local copies, waits for them, and re-layouts  0.88 us (2%)
    pallas_call x1, Pallas kernels, on_device(): pl.pallas_call(body, out_shape=vmem((BANDS, PH, PW), f32), in_specs=[pl.B...  44.8 us

profile of v4, /device:TPU:1, one launch (start us, length us, event | category | flops | bytes accessed | tf_op | source)
XLA Modules:
  0.0 45.7 jit_solution(5781607240896042243)
XLA Ops:
  0.0 44.8 %shard_map.91 = f32[6,128,256]{2,1,0:T(8,128)S(1)} custom-call(f32[128,8,256]{2,1,0:T(8,128)} %pix_hbm.1, bf16[128,8,256]{2,1,0:T(8,128)(2,1)} %ivar_hbm.1, s32[128,8,256]{2,1,0:T(8,128)} %mask_hbm.1, s32[1,128]{1,0:T(1,128)} %bitcast.6, s32[1,128]{1,0:T(1,128)} %bitcast.7, s32[1,128]{1,0:T(1,128)} %bitcast.8, s32[1,96]{1,0:T(1,128)} %bitcast.9, ...), custom_call_target="tpu_custom_call" | custom-call | flops 6442450944 | bytes 4194304 | tf_op jit(solution)/shard_map/pallas_call | solution.py:424
  44.8 0.9 %copy.11 = f32[6,128,256]{2,1,0:T(8,128)} copy(f32[6,128,256]{2,1,0:T(8,128)S(1)} %shard_map.91) | data formatting | bytes 1572864

commit v5 on v4

--- a/solution.py
+++ b/solution.py
@@ -27,6 +27,7 @@
 ROWS = PH + 64
 FIRST = 32 - HALF
 OUT_ROWS = 528
+LAST = 4 * (32 + PH + HALF)
 
 
 def iota(shape, dim):
@@ -62,12 +63,14 @@
     data_in,
     sums,
     weights,
-    mean_b,
+    ends,
+    ends_b,
     packs,
     above,
     below,
     side_l,
     side_r,
+    corner,
     image32,
     image2,
     full,
@@ -274,15 +277,6 @@
             else:
                 sums[b] = part
 
-    pltpu.make_async_remote_copy(
-        src_ref=data.at[pl.ds(0, 127 * 16)], dst_ref=data_in.at[pl.ds(0, 127 * 16)], send_sem=data_send,
-        recv_sem=data_recv.at[0], device_id=(col ^ 1, row), device_id_type=MESH,
-    ).wait_send()
-    pltpu.make_async_remote_copy(
-        src_ref=label.at[pl.ds(0, 127)], dst_ref=label_in.at[pl.ds(0, 127)], send_sem=label_send,
-        recv_sem=label_recv.at[0], device_id=(col ^ 1, row), device_id_type=MESH,
-    ).wait_send()
-
     up, down = (row + 15) & 15, (row + 1) & 15
     left, right = (col + 7) & 7, (col + 1) & 7
 
@@ -298,9 +292,8 @@
     for b in range(BANDS):
         mean = sums[b, :, 0:PW] / jnp.maximum(sums[b, :, PW : 2 * PW], 1.0)
         sums[b, :, 0:PW] = mean
-        mean_b[b] = mean.astype(jnp.bfloat16)
-        halo(mean_b.at[b, PH - 32 : PH], above.at[b], 0, (col, down)).start()
-        halo(mean_b.at[b, 0:32], below.at[b], 1, (col, up)).start()
+        ends[0, b * HALF : (b + 1) * HALF] = mean[PH - HALF : PH]
+        ends[1, b * HALF : (b + 1) * HALF] = mean[0:HALF]
         here = (lane_p >= b * HALF) & (lane_p < (b + 1) * HALF)
         pack_l = jnp.where(here, pltpu.roll(mean[:, 0:128], b * HALF, 1), pack_l)
         pack_r = jnp.where(here, pltpu.roll(mean[:, 128:256], (b * HALF + HALF) % 128, 1), pack_r)
@@ -316,7 +309,12 @@
         halo(packs.at[0, 0:32], side_r.at[32 + PH : ROWS], 6, (left, up)),
         halo(packs.at[1, 0:32], side_l.at[32 + PH : ROWS], 7, (right, up)),
     ]
-    for copy in sides + corners:
+    for copy in corners + sides:
+        copy.start()
+    ends[:, BANDS * HALF :] = jnp.zeros_like(ends[:, BANDS * HALF :])
+    ends_b[...] = ends[...].astype(jnp.bfloat16)
+    rows = [halo(ends_b.at[0], above, 0, (col, down)), halo(ends_b.at[1], below, 1, (col, up))]
+    for copy in rows:
         copy.start()
 
     has_up, has_down, has_left, has_right = row > 0, row < 15, col > 0, col < 7
@@ -377,8 +375,9 @@
 
     for b in range(BANDS):
         inner_windows(b, sums[b, :, 0:128], sums[b, :, 128:256], 32)
+        image32[b, LAST : LAST + 32] = jnp.zeros((32, 128), jnp.float32)
     for copy in sides:
-        copy.wait()
+        copy.wait_recv()
     for b in range(BANDS):
         outer_windows(
             b, sums[b, :, 0:128], sums[b, :, 128:256], side_l[32 : 32 + PH], side_r[32 : 32 + PH], 32
@@ -387,22 +386,42 @@
         matmul(b, ((80, 432),))
         finish(b, 24, 104)
 
+    for copy in rows:
+        copy.wait_recv()
+    strips = ((0, 32 - HALF, 32 - HALF), (1, 0, 32 + PH))
+    ends[0] = jnp.where(has_up, above[...].astype(jnp.float32), 0.0)
+    ends[1] = jnp.where(has_down, below[...].astype(jnp.float32), 0.0)
+    for b in range(BANDS):
+        for i, _, first in strips:
+            strip = ends[i, b * HALF : (b + 1) * HALF]
+            inner_windows(b, strip[:, 0:128], strip[:, 128:256], first)
     for copy in corners:
-        copy.wait()
-    halo(mean_b.at[:, PH - 32 : PH], above, 0, (col, down)).wait()
-    halo(mean_b.at[:, 0:32], below, 1, (col, up)).wait()
+        copy.wait_recv()
+    for i, here, first in ((0, has_up, 0), (1, has_down, 32 + PH)):
+        corner[i, 0] = jnp.where(here, side_l[first : first + 32].astype(jnp.float32), 0.0)
+        corner[i, 1] = jnp.where(here, side_r[first : first + 32].astype(jnp.float32), 0.0)
     for b in range(BANDS):
-        for ref, here, first, side in ((above, has_up, 0, 0), (below, has_down, 32 + PH, 32 + PH)):
-            rows = jnp.where(here, ref[b].astype(jnp.float32), 0.0)
-            edge_l = jnp.where(here, side_l[side : side + 32].astype(jnp.float32), 0.0)
-            edge_r = jnp.where(here, side_r[side : side + 32].astype(jnp.float32), 0.0)
-            inner_windows(b, rows[:, 0:128], rows[:, 128:256], first)
-            outer_windows(b, rows[:, 0:128], rows[:, 128:256], edge_l, edge_r, first)
+        for i, at, first in strips:
+            strip = ends[i, b * HALF : (b + 1) * HALF]
+            outer_windows(
+                b, strip[:, 0:128], strip[:, 128:256], corner[i, 0, at : at + HALF], corner[i, 1, at : at + HALF], first
+            )
         widen(b, 48, 128, 48, 128)
         widen(b, 640, 736, 608, 736)
         matmul(b, ((0, 80), (432, OUT_ROWS)))
         finish(b, 0, 24)
         finish(b, 104, 128)
+
+    for copy in sides + rows + corners:
+        copy.wait_send()
+    pltpu.make_async_remote_copy(
+        src_ref=data.at[pl.ds(0, 127 * 16)], dst_ref=data_in.at[pl.ds(0, 127 * 16)], send_sem=data_send,
+        recv_sem=data_recv.at[0], device_id=(col ^ 1, row), device_id_type=MESH,
+    ).wait_send()
+    pltpu.make_async_remote_copy(
+        src_ref=label.at[pl.ds(0, 127)], dst_ref=label_in.at[pl.ds(0, 127)], send_sem=label_send,
+        recv_sem=label_recv.at[0], device_id=(col ^ 1, row), device_id_type=MESH,
+    ).wait_send()
 
 
 def on_device(
@@ -445,12 +464,14 @@
             vmem((2048, 2 * PW), bf16),
             vmem((BANDS, PH, 2 * PW), f32),
             vmem((BANDS, GROUP * TILE, SHIFTS * 128), bf16),
-            vmem((BANDS, PH, PW), bf16),
+            vmem((2, 128, PW), f32),
+            vmem((2, 128, PW), bf16),
             vmem((2, PH, 128), bf16),
-            vmem((BANDS, 32, PW), bf16),
-            vmem((BANDS, 32, PW), bf16),
+            vmem((128, PW), bf16),
+            vmem((128, PW), bf16),
             vmem((ROWS, 128), bf16),
             vmem((ROWS, 128), bf16),
+            vmem((2, 2, 32, 128), f32),
             vmem((BANDS, 4 * ROWS + 8, 128), f32),
             vmem((BANDS, 4 * ROWS, 256), bf16),
             vmem((BANDS, OUT_ROWS, 256), f32),

time: 46.2 us -> 45 us (0.974)
  Pallas kernels: 44.8 us -> 43.9 us
    pallas_call x1, Pallas kernels: 44.8 us -> 43.9 us  [on_device(): pl.pallas_call(body, out_shape=vmem((BANDS, PH, PW), f32), in_specs=[pl.B...]
where the time goes in v5:
time: 45 us; the launch traced here: 44.8 us
  Pallas kernels  43.9 us (98%)
  local copies, waits for them, and re-layouts  0.88 us (2%)
    pallas_call x1, Pallas kernels, on_device(): pl.pallas_call(body, out_shape=vmem((BANDS, PH, PW), f32), in_specs=[pl.B...  43.9 us

profile of v5, /device:TPU:1, one launch (start us, length us, event | category | flops | bytes accessed | tf_op | source)
XLA Modules:
  0.0 44.8 jit_solution(12132185404820123916)
XLA Ops:
  0.0 43.9 %shard_map.91 = f32[6,128,256]{2,1,0:T(8,128)S(1)} custom-call(f32[128,8,256]{2,1,0:T(8,128)} %pix_hbm.1, bf16[128,8,256]{2,1,0:T(8,128)(2,1)} %ivar_hbm.1, s32[128,8,256]{2,1,0:T(8,128)} %mask_hbm.1, s32[1,128]{1,0:T(1,128)} %bitcast.6, s32[1,128]{1,0:T(1,128)} %bitcast.7, s32[1,128]{1,0:T(1,128)} %bitcast.8, s32[1,96]{1,0:T(1,128)} %bitcast.9, ...), custom_call_target="tpu_custom_call" | custom-call | flops 6442450944 | bytes 4194304 | tf_op jit(solution)/shard_map/pallas_call | solution.py:443
  43.9 0.9 %copy.11 = f32[6,128,256]{2,1,0:T(8,128)} copy(f32[6,128,256]{2,1,0:T(8,128)S(1)} %shard_map.91) | data formatting | bytes 1572864

commit v6 on v5

--- a/solution.py
+++ b/solution.py
@@ -14,10 +14,10 @@
 BH = 8
 MESH = pl.DeviceIdType.MESH
 
-STEP_X = (-2134884224, -1862789622, 1547504322, -997211824, 1521461850, -1521111046, -2790657, 930528599)
-STEP_Y = (-1473245152, 621707680, 130240700, 824245269, -1347790166, 1516198495, 2105372591, 904625533)
-STEP_Z = (672072970, 1252255834, -246087895, 998725, -84236886, 1437267365, -715665414, 15743)
-STEP_C = (285475844, 71372868, 1091585041, 1431572740, 1145324612, 1145324612, 286331972, 357912849)
+STEP_X = (-1610415072, 884100632, -1941376697, -997440312, -1782682714, -373949073, 1810198426, 930526717)
+STEP_Y = (671138056, -852716666, 304233553, 824382227, 1734851178, -1699252357, 1859770862, 904623991)
+STEP_Z = (-1999097790, 1405692129, 1805307164, 1006974, 1524231834, -1497901570, -812206469, 14293)
+STEP_C = (22282240, 0, 1431633920, 1431655765, 0, 1430257664, 1431655765, 357913941)
 LINES, PLANES = 13, 64
 
 GROUP = 4

time: 45 us -> 44.3 us (0.984)
  Pallas kernels: 43.9 us -> 43.3 us
    pallas_call x1, Pallas kernels: 43.9 us -> 43.3 us  [on_device(): pl.pallas_call(body, out_shape=vmem((BANDS, PH, PW), f32), in_specs=[pl.B...]
where the time goes in v6:
time: 44.3 us; the launch traced here: 44.2 us
  Pallas kernels  43.3 us (98%)
  local copies, waits for them, and re-layouts  0.88 us (2%)
    pallas_call x1, Pallas kernels, on_device(): pl.pallas_call(body, out_shape=vmem((BANDS, PH, PW), f32), in_specs=[pl.B...  43.3 us

profile of v6, /device:TPU:1, one launch (start us, length us, event | category | flops | bytes accessed | tf_op | source)
XLA Modules:
  0.0 44.2 jit_solution(13044944460911198252)
XLA Ops:
  0.0 43.3 %shard_map.91 = f32[6,128,256]{2,1,0:T(8,128)S(1)} custom-call(f32[128,8,256]{2,1,0:T(8,128)} %pix_hbm.1, bf16[128,8,256]{2,1,0:T(8,128)(2,1)} %ivar_hbm.1, s32[128,8,256]{2,1,0:T(8,128)} %mask_hbm.1, s32[1,128]{1,0:T(1,128)} %bitcast.6, s32[1,128]{1,0:T(1,128)} %bitcast.7, s32[1,128]{1,0:T(1,128)} %bitcast.8, s32[1,96]{1,0:T(1,128)} %bitcast.9, ...), custom_call_target="tpu_custom_call" | custom-call | flops 6442450944 | bytes 4194304 | tf_op jit(solution)/shard_map/pallas_call | solution.py:443
  43.3 0.9 %copy.11 = f32[6,128,256]{2,1,0:T(8,128)} copy(f32[6,128,256]{2,1,0:T(8,128)S(1)} %shard_map.91) | data formatting | bytes 1572864

commit v7 on v6

--- a/solution.py
+++ b/solution.py
@@ -14,10 +14,10 @@
 BH = 8
 MESH = pl.DeviceIdType.MESH
 
-STEP_X = (-1610415072, 884100632, -1941376697, -997440312, -1782682714, -373949073, 1810198426, 930526717)
-STEP_Y = (671138056, -852716666, 304233553, 824382227, 1734851178, -1699252357, 1859770862, 904623991)
-STEP_Z = (-1999097790, 1405692129, 1805307164, 1006974, 1524231834, -1497901570, -812206469, 14293)
-STEP_C = (22282240, 0, 1431633920, 1431655765, 0, 1430257664, 1431655765, 357913941)
+STEP_X = (537068576, 823337521, 1310237458, -246991694, -1782682714, -373949073, 1810198426, 930526717)
+STEP_Y = (-2013216504, -1941156792, -1819924284, 1011993900, 1734851178, -1699252357, 1859770862, 904623991)
+STEP_Z = (1758998594, 1031141806, 685869056, -853781559, 1524231834, -1497901570, -812206469, 14293)
+STEP_C = (1431568384, 1431655765, 341, 0, 0, 1430257664, 1431655765, 357913941)
 LINES, PLANES = 13, 64
 
 GROUP = 4
@@ -286,6 +286,20 @@
             device_id=target, device_id_type=MESH,
         )
 
+    has_up, has_down, has_left, has_right = row > 0, row < 15, col > 0, col < 7
+
+    def start(copies):
+        for copy, sends, _ in copies:
+            pl.when(sends)(copy.start)
+
+    def arrive(copies):
+        for copy, _, receives in copies:
+            pl.when(receives)(copy.wait_recv)
+
+    def leave(copies):
+        for copy, sends, _ in copies:
+            pl.when(sends)(copy.wait_send)
+
     lane_p = iota((PH, 128), 1)
     pack_l = jnp.zeros((PH, 128), jnp.float32)
     pack_r = jnp.zeros((PH, 128), jnp.float32)
@@ -300,24 +314,40 @@
     packs[0] = pack_l.astype(jnp.bfloat16)
     packs[1] = pack_r.astype(jnp.bfloat16)
     sides = [
-        halo(packs.at[0], side_r.at[32 : 32 + PH], 2, (left, row)),
-        halo(packs.at[1], side_l.at[32 : 32 + PH], 3, (right, row)),
+        (halo(packs.at[0], side_r.at[32 : 32 + PH], 2, (left, row)), has_left, has_right),
+        (halo(packs.at[1], side_l.at[32 : 32 + PH], 3, (right, row)), has_right, has_left),
     ]
     corners = [
-        halo(packs.at[0, PH - 32 : PH], side_r.at[0:32], 4, (left, down)),
-        halo(packs.at[1, PH - 32 : PH], side_l.at[0:32], 5, (right, down)),
-        halo(packs.at[0, 0:32], side_r.at[32 + PH : ROWS], 6, (left, up)),
-        halo(packs.at[1, 0:32], side_l.at[32 + PH : ROWS], 7, (right, up)),
+        (
+            halo(packs.at[0, PH - 32 : PH], side_r.at[0:32], 4, (left, down)),
+            has_left & has_down,
+            has_right & has_up,
+        ),
+        (
+            halo(packs.at[1, PH - 32 : PH], side_l.at[0:32], 5, (right, down)),
+            has_right & has_down,
+            has_left & has_up,
+        ),
+        (
+            halo(packs.at[0, 0:32], side_r.at[32 + PH : ROWS], 6, (left, up)),
+            has_left & has_up,
+            has_right & has_down,
+        ),
+        (
+            halo(packs.at[1, 0:32], side_l.at[32 + PH : ROWS], 7, (right, up)),
+            has_right & has_up,
+            has_left & has_down,
+        ),
     ]
-    for copy in corners + sides:
-        copy.start()
+    start(corners + sides)
     ends[:, BANDS * HALF :] = jnp.zeros_like(ends[:, BANDS * HALF :])
     ends_b[...] = ends[...].astype(jnp.bfloat16)
-    rows = [halo(ends_b.at[0], above, 0, (col, down)), halo(ends_b.at[1], below, 1, (col, up))]
-    for copy in rows:
-        copy.start()
-
-    has_up, has_down, has_left, has_right = row > 0, row < 15, col > 0, col < 7
+    rows = [
+        (halo(ends_b.at[0], above, 0, (col, down)), has_down, has_up),
+        (halo(ends_b.at[1], below, 1, (col, up)), has_up, has_down),
+    ]
+    start(rows)
+
 
     def inner_windows(b, tile0, tile1, first):
         rows = tile0.shape[0]
@@ -376,8 +406,7 @@
     for b in range(BANDS):
         inner_windows(b, sums[b, :, 0:128], sums[b, :, 128:256], 32)
         image32[b, LAST : LAST + 32] = jnp.zeros((32, 128), jnp.float32)
-    for copy in sides:
-        copy.wait_recv()
+    arrive(sides)
     for b in range(BANDS):
         outer_windows(
             b, sums[b, :, 0:128], sums[b, :, 128:256], side_l[32 : 32 + PH], side_r[32 : 32 + PH], 32
@@ -386,8 +415,7 @@
         matmul(b, ((80, 432),))
         finish(b, 24, 104)
 
-    for copy in rows:
-        copy.wait_recv()
+    arrive(rows)
     strips = ((0, 32 - HALF, 32 - HALF), (1, 0, 32 + PH))
     ends[0] = jnp.where(has_up, above[...].astype(jnp.float32), 0.0)
     ends[1] = jnp.where(has_down, below[...].astype(jnp.float32), 0.0)
@@ -395,8 +423,7 @@
         for i, _, first in strips:
             strip = ends[i, b * HALF : (b + 1) * HALF]
             inner_windows(b, strip[:, 0:128], strip[:, 128:256], first)
-    for copy in corners:
-        copy.wait_recv()
+    arrive(corners)
     for i, here, first in ((0, has_up, 0), (1, has_down, 32 + PH)):
         corner[i, 0] = jnp.where(here, side_l[first : first + 32].astype(jnp.float32), 0.0)
         corner[i, 1] = jnp.where(here, side_r[first : first + 32].astype(jnp.float32), 0.0)
@@ -412,8 +439,7 @@
         finish(b, 0, 24)
         finish(b, 104, 128)
 
-    for copy in sides + rows + corners:
-        copy.wait_send()
+    leave(sides + rows + corners)
     pltpu.make_async_remote_copy(
         src_ref=data.at[pl.ds(0, 127 * 16)], dst_ref=data_in.at[pl.ds(0, 127 * 16)], send_sem=data_send,
         recv_sem=data_recv.at[0], device_id=(col ^ 1, row), device_id_type=MESH,

time: 44.3 us -> 44.2 us (level)
  no operation moved by 1% of the time
where the time goes in v7:
time: 44.2 us; the launch traced here: 44 us
  Pallas kernels  43.1 us (98%)
  local copies, waits for them, and re-layouts  0.88 us (2%)
    pallas_call x1, Pallas kernels, on_device(): pl.pallas_call(body, out_shape=vmem((BANDS, PH, PW), f32), in_specs=[pl.B...  43.1 us

profile of v7, /device:TPU:1, one launch (start us, length us, event | category | flops | bytes accessed | tf_op | source)
XLA Modules:
  0.0 44.0 jit_solution(12510673909438652921)
XLA Ops:
  0.0 43.1 %shard_map.91 = f32[6,128,256]{2,1,0:T(8,128)S(1)} custom-call(f32[128,8,256]{2,1,0:T(8,128)} %pix_hbm.1, bf16[128,8,256]{2,1,0:T(8,128)(2,1)} %ivar_hbm.1, s32[128,8,256]{2,1,0:T(8,128)} %mask_hbm.1, s32[1,128]{1,0:T(1,128)} %bitcast.6, s32[1,128]{1,0:T(1,128)} %bitcast.7, s32[1,128]{1,0:T(1,128)} %bitcast.8, s32[1,96]{1,0:T(1,128)} %bitcast.9, ...), custom_call_target="tpu_custom_call" | custom-call | flops 6442450944 | bytes 4194304 | tf_op jit(solution)/shard_map/pallas_call | solution.py:469
  43.1 0.9 %copy.11 = f32[6,128,256]{2,1,0:T(8,128)} copy(f32[6,128,256]{2,1,0:T(8,128)S(1)} %shard_map.91) | data formatting | bytes 1572864

commit v8 on v7

--- a/solution.py
+++ b/solution.py
@@ -425,8 +425,8 @@
             inner_windows(b, strip[:, 0:128], strip[:, 128:256], first)
     arrive(corners)
     for i, here, first in ((0, has_up, 0), (1, has_down, 32 + PH)):
-        corner[i, 0] = jnp.where(here, side_l[first : first + 32].astype(jnp.float32), 0.0)
-        corner[i, 1] = jnp.where(here, side_r[first : first + 32].astype(jnp.float32), 0.0)
+        corner[i, 0, 0:32] = jnp.where(here, side_l[first : first + 32].astype(jnp.float32), 0.0)
+        corner[i, 1, 0:32] = jnp.where(here, side_r[first : first + 32].astype(jnp.float32), 0.0)
     for b in range(BANDS):
         for i, at, first in strips:
             strip = ends[i, b * HALF : (b + 1) * HALF]
@@ -481,7 +481,7 @@
             vmem((1, exposure_band.size), i32),
             vmem(basis.shape, f32),
             smem(scales.shape, f32),
-            vmem((TAPS, 128), f32),
+            vmem((TAPS + 4, 128), f32),
             vmem((8, 128), i32),
             smem((8, 128), i32),
             vmem((128, 128), i32),
@@ -497,7 +497,7 @@
             vmem((128, PW), bf16),
             vmem((ROWS, 128), bf16),
             vmem((ROWS, 128), bf16),
-            vmem((2, 2, 32, 128), f32),
+            vmem((2, 2, 48, 128), f32),
             vmem((BANDS, 4 * ROWS + 8, 128), f32),
             vmem((BANDS, 4 * ROWS, 256), bf16),
             vmem((BANDS, OUT_ROWS, 256), f32),

time: 44.2 us -> 44.1 us (level)
  no operation moved by 1% of the time
where the time goes in v8:
time: 44.1 us; the launch traced here: 44 us
  Pallas kernels  43.1 us (98%)
  local copies, waits for them, and re-layouts  0.88 us (2%)
    pallas_call x1, Pallas kernels, on_device(): pl.pallas_call(body, out_shape=vmem((BANDS, PH, PW), f32), in_specs=[pl.B...  43.1 us
    unnamed x1, local copies, waits for them, and re-layouts  0.88 us

profile of v8, /device:TPU:1, one launch (start us, length us, event | category | flops | bytes accessed | tf_op | source)
XLA Modules:
  0.0 44.0 jit_solution(9698812788503296282)
XLA Ops:
  0.0 43.1 %shard_map.91 = f32[6,128,256]{2,1,0:T(8,128)S(1)} custom-call(f32[128,8,256]{2,1,0:T(8,128)} %pix_hbm.1, bf16[128,8,256]{2,1,0:T(8,128)(2,1)} %ivar_hbm.1, s32[128,8,256]{2,1,0:T(8,128)} %mask_hbm.1, s32[1,128]{1,0:T(1,128)} %bitcast.6, s32[1,128]{1,0:T(1,128)} %bitcast.7, s32[1,128]{1,0:T(1,128)} %bitcast.8, s32[1,96]{1,0:T(1,128)} %bitcast.9, ...), custom_call_target="tpu_custom_call" | custom-call | flops 6442450944 | bytes 4194304 | tf_op jit(solution)/shard_map/pallas_call | solution.py:469
  43.1 0.9 %copy.11 = f32[6,128,256]{2,1,0:T(8,128)} copy(f32[6,128,256]{2,1,0:T(8,128)S(1)} %shard_map.91) | data formatting | bytes 1572864
